TPU v7x, 512 devices: a whole 4x4x16 slice. The times are simulated.
512 devices in a mesh: sta: 64 (over z_lo, x, core), win: 8 (over y, z_hi).
Axes of the slice: x: 4, y: 4, z: 16 (z_hi: 2, z_lo: 8; z = z_hi * 8 + z_lo), core: 2. Of those that a mesh axis runs over, the one named last changes fastest.
Arguments:
- spectra: bfloat16 [2, 8, 256, 2048], P(None, 'win', 'sta'), may hold values from -500 to 500
- quality: int32 [8, 256], P('win', 'sta'), may hold values 0 or 1
- block_mask: int32 [64, 64], P('sta'), may hold values 0 or 1
Outputs:
- correlations: bfloat16 [256, 256, 256], P('sta', 'win')
All inputs are finite; a program needn't handle non-finite values. No bound on the sum of `quality` or of `block_mask` on one device may be relied on, other than what follows from the above.
Results may differ from a plain program's by a relative error of at most 0.0066.
Values may be sent and summed in bfloat16 or wider, within the bound.
No kernel may reach another device: no remote copies, remote signals or barrier semaphores. Data moves between devices by JAX's collectives and lax.ppermute only.
A program may use at most 64 MiB of HBM per device.

v0:
```python
import math

import jax
import jax.numpy as jnp
from jax import lax
from jax.sharding import PartitionSpec as P

LAGS = 256


def passed_along(array, axis, by):
    devices = lax.axis_size(axis)
    return lax.ppermute(array, axis, [(i, (i + by) % devices) for i in range(devices)])


def whiten(spectra, quality):
    values = spectra.astype(jnp.float32)
    power_mean = jnp.mean(values[0] * values[0] + values[1] * values[1], axis=-1, keepdims=True)
    flags = quality.astype(jnp.float32)[:, :, None]
    return (values * (lax.rsqrt(power_mean + 1e-06) * flags)[None]).astype(jnp.bfloat16)


def lag_table(bins_count, lag_count):
    freq_index = jnp.arange(bins_count, dtype=jnp.int32)[:, None]
    lag_index = jnp.arange(lag_count, dtype=jnp.int32)[None, :] - lag_count // 2
    phase = freq_index * lag_index % (2 * bins_count)
    angles = phase.astype(jnp.float32) * jnp.float32(math.pi / bins_count)
    norm_scale = jnp.float32(1.0 / math.sqrt(bins_count))
    stacked = jnp.concatenate([jnp.cos(angles), -jnp.sin(angles)], axis=0) * norm_scale
    return stacked.astype(jnp.bfloat16)


def cross_block(own_white, far_piece):
    own_float = own_white.astype(jnp.float32)
    per_block = own_white.shape[2]
    blocks_in = far_piece.shape[2] // per_block
    far_float = far_piece.astype(jnp.float32).reshape(
        2, far_piece.shape[1], blocks_in, per_block, far_piece.shape[3]
    )
    real_part = jnp.einsum("wif,wbjf->ibjf", own_float[0], far_float[0]) + jnp.einsum(
        "wif,wbjf->ibjf", own_float[1], far_float[1]
    )
    imag_part = jnp.einsum("wif,wbjf->ibjf", own_float[1], far_float[0]) - jnp.einsum(
        "wif,wbjf->ibjf", own_float[0], far_float[1]
    )
    return jnp.concatenate([real_part, imag_part], axis=-1).astype(jnp.bfloat16)


def transform(cross_spec, basis_table):
    leading = cross_spec.shape[:-1]
    flat = jnp.dot(
        cross_spec.reshape(-1, cross_spec.shape[-1]),
        basis_table,
        preferred_element_type=jnp.float32,
    )
    return flat.reshape(leading + (basis_table.shape[1],))


def shards(spectra, quality, block_mask):
    sta_count = lax.axis_size("sta")
    my_block = lax.axis_index("sta")
    own_white = whiten(spectra, quality)
    bins_count = spectra.shape[3]
    per_block = spectra.shape[2]
    basis_table = lag_table(bins_count, LAGS)
    zero_index = jnp.int32(0)
    initial = jnp.zeros((per_block, sta_count, per_block, 2 * bins_count), jnp.bfloat16)

    def place(stack_buffer, far_piece, first_block):
        cross_spec = cross_block(own_white, far_piece)
        starts = (zero_index, first_block, zero_index, zero_index)
        return lax.dynamic_update_slice(stack_buffer, cross_spec, starts)

    def advance(offset, loop_state):
        stack_buffer, partner = loop_state
        partner = passed_along(partner, "sta", 1)
        stack_buffer = place(stack_buffer, partner, (my_block - offset) % sta_count)
        return (stack_buffer, partner)

    stack_buffer = place(initial, own_white, my_block)
    stack_buffer, _ = lax.fori_loop(1, sta_count, advance, (stack_buffer, own_white))
    correlation = transform(stack_buffer, basis_table)
    pair_mask = block_mask[0].astype(jnp.float32)
    correlation = correlation * pair_mask[None, :, None, None]
    correlation = correlation.reshape(per_block, sta_count * per_block, LAGS)
    summed = lax.psum_scatter(correlation, "win", scatter_dimension=1, tiled=True)
    return summed.astype(jnp.bfloat16)


def solution(mesh):
    placed = (P(None, "win", "sta", None), P("win", "sta"), P("sta", None))
    return jax.shard_map(
        shards, mesh=mesh, in_specs=placed, out_specs=P("sta", "win", None), check_vma=False
    )
```

profile of v0, /device:TPU:24, one launch (start us, length us, event | category | flops | bytes accessed | tf_op | source)
XLA Modules:
  0.0 1127.3 jit_solution(10379828104085921690)
XLA Ops:
  10.7 945.9 %while.17 = (s32[]{:T(128)}, bf16[4,64,4,4096]{3,2,1,0:T(4,128)(2,1)}, bf16[2,1,4,2048]{3,2,1,0:T(4,128)(2,1)S(1)}, bf16[2,1,4,2048]{3,2,1,0:T(4,128)(2,1)S(1)},...) while((s32[]{:T(128)}, bf16[4,64,4,4096]{3,2,1,0:T(4,128)(2,1)}, ...), condition=%wide.region_2.3_spmd, body=%wide.region_1.2_spmd.sunk | while | flops 557073 | bytes 917796 | solution.py:81
  12.7 14.5 %collective-permute-done = bf16[2,1,4,2048]{3,2,1,0:T(4,128)(2,1)S(1)} collective-permute-done((bf16[2,1,4,2048]{3,2,1,0:T(4,128)(2,1)S(1)}, bf16[2,1,4,2048]{3,2,1,0:T(4,128)(2,1)S(1)}, u32[]{:S(2)}, u32[]{:S(2)}) %collective-permute-start) | collective-permute-done | bytes 32800 | tf_op jit(solution)/shard_map/while/body/eval_jaxpr/ppermute | solution.py:13
  29.9 12.0 %collective-permute-done = bf16[2,1,4,2048]{3,2,1,0:T(4,128)(2,1)S(1)} collective-permute-done((bf16[2,1,4,2048]{3,2,1,0:T(4,128)(2,1)S(1)}, bf16[2,1,4,2048]{3,2,1,0:T(4,128)(2,1)S(1)}, u32[]{:S(2)}, u32[]{:S(2)}) %collective-permute-start) | collective-permute-done | bytes 32800 | tf_op jit(solution)/shard_map/while/body/eval_jaxpr/ppermute | solution.py:13
  44.7 12.0 %collective-permute-done = bf16[2,1,4,2048]{3,2,1,0:T(4,128)(2,1)S(1)} collective-permute-done((bf16[2,1,4,2048]{3,2,1,0:T(4,128)(2,1)S(1)}, bf16[2,1,4,2048]{3,2,1,0:T(4,128)(2,1)S(1)}, u32[]{:S(2)}, u32[]{:S(2)}) %collective-permute-start) | collective-permute-done | bytes 32800 | tf_op jit(solution)/shard_map/while/body/eval_jaxpr/ppermute | solution.py:13
  59.5 12.0 %collective-permute-done = bf16[2,1,4,2048]{3,2,1,0:T(4,128)(2,1)S(1)} collective-permute-done((bf16[2,1,4,2048]{3,2,1,0:T(4,128)(2,1)S(1)}, bf16[2,1,4,2048]{3,2,1,0:T(4,128)(2,1)S(1)}, u32[]{:S(2)}, u32[]{:S(2)}) %collective-permute-start) | collective-permute-done | bytes 32800 | tf_op jit(solution)/shard_map/while/body/eval_jaxpr/ppermute | solution.py:13
  74.2 12.0 %collective-permute-done = bf16[2,1,4,2048]{3,2,1,0:T(4,128)(2,1)S(1)} collective-permute-done((bf16[2,1,4,2048]{3,2,1,0:T(4,128)(2,1)S(1)}, bf16[2,1,4,2048]{3,2,1,0:T(4,128)(2,1)S(1)}, u32[]{:S(2)}, u32[]{:S(2)}) %collective-permute-start) | collective-permute-done | bytes 32800 | tf_op jit(solution)/shard_map/while/body/eval_jaxpr/ppermute | solution.py:13
  89.0 12.0 %collective-permute-done = bf16[2,1,4,2048]{3,2,1,0:T(4,128)(2,1)S(1)} collective-permute-done((bf16[2,1,4,2048]{3,2,1,0:T(4,128)(2,1)S(1)}, bf16[2,1,4,2048]{3,2,1,0:T(4,128)(2,1)S(1)}, u32[]{:S(2)}, u32[]{:S(2)}) %collective-permute-start) | collective-permute-done | bytes 32800 | tf_op jit(solution)/shard_map/while/body/eval_jaxpr/ppermute | solution.py:13
  103.8 12.0 %collective-permute-done = bf16[2,1,4,2048]{3,2,1,0:T(4,128)(2,1)S(1)} collective-permute-done((bf16[2,1,4,2048]{3,2,1,0:T(4,128)(2,1)S(1)}, bf16[2,1,4,2048]{3,2,1,0:T(4,128)(2,1)S(1)}, u32[]{:S(2)}, u32[]{:S(2)}) %collective-permute-start) | collective-permute-done | bytes 32800 | tf_op jit(solution)/shard_map/while/body/eval_jaxpr/ppermute | solution.py:13
  118.5 12.0 %collective-permute-done = bf16[2,1,4,2048]{3,2,1,0:T(4,128)(2,1)S(1)} collective-permute-done((bf16[2,1,4,2048]{3,2,1,0:T(4,128)(2,1)S(1)}, bf16[2,1,4,2048]{3,2,1,0:T(4,128)(2,1)S(1)}, u32[]{:S(2)}, u32[]{:S(2)}) %collective-permute-start) | collective-permute-done | bytes 32800 | tf_op jit(solution)/shard_map/while/body/eval_jaxpr/ppermute | solution.py:13
  133.3 12.0 %collective-permute-done = bf16[2,1,4,2048]{3,2,1,0:T(4,128)(2,1)S(1)} collective-permute-done((bf16[2,1,4,2048]{3,2,1,0:T(4,128)(2,1)S(1)}, bf16[2,1,4,2048]{3,2,1,0:T(4,128)(2,1)S(1)}, u32[]{:S(2)}, u32[]{:S(2)}) %collective-permute-start) | collective-permute-done | bytes 32800 | tf_op jit(solution)/shard_map/while/body/eval_jaxpr/ppermute | solution.py:13
  148.1 12.0 %collective-permute-done = bf16[2,1,4,2048]{3,2,1,0:T(4,128)(2,1)S(1)} collective-permute-done((bf16[2,1,4,2048]{3,2,1,0:T(4,128)(2,1)S(1)}, bf16[2,1,4,2048]{3,2,1,0:T(4,128)(2,1)S(1)}, u32[]{:S(2)}, u32[]{:S(2)}) %collective-permute-start) | collective-permute-done | bytes 32800 | tf_op jit(solution)/shard_map/while/body/eval_jaxpr/ppermute | solution.py:13
  162.8 12.0 %collective-permute-done = bf16[2,1,4,2048]{3,2,1,0:T(4,128)(2,1)S(1)} collective-permute-done((bf16[2,1,4,2048]{3,2,1,0:T(4,128)(2,1)S(1)}, bf16[2,1,4,2048]{3,2,1,0:T(4,128)(2,1)S(1)}, u32[]{:S(2)}, u32[]{:S(2)}) %collective-permute-start) | collective-permute-done | bytes 32800 | tf_op jit(solution)/shard_map/while/body/eval_jaxpr/ppermute | solution.py:13
  177.6 12.0 %collective-permute-done = bf16[2,1,4,2048]{3,2,1,0:T(4,128)(2,1)S(1)} collective-permute-done((bf16[2,1,4,2048]{3,2,1,0:T(4,128)(2,1)S(1)}, bf16[2,1,4,2048]{3,2,1,0:T(4,128)(2,1)S(1)}, u32[]{:S(2)}, u32[]{:S(2)}) %collective-permute-start) | collective-permute-done | bytes 32800 | tf_op jit(solution)/shard_map/while/body/eval_jaxpr/ppermute | solution.py:13
  192.4 12.0 %collective-permute-done = bf16[2,1,4,2048]{3,2,1,0:T(4,128)(2,1)S(1)} collective-permute-done((bf16[2,1,4,2048]{3,2,1,0:T(4,128)(2,1)S(1)}, bf16[2,1,4,2048]{3,2,1,0:T(4,128)(2,1)S(1)}, u32[]{:S(2)}, u32[]{:S(2)}) %collective-permute-start) | collective-permute-done | bytes 32800 | tf_op jit(solution)/shard_map/while/body/eval_jaxpr/ppermute | solution.py:13
  207.1 12.0 %collective-permute-done = bf16[2,1,4,2048]{3,2,1,0:T(4,128)(2,1)S(1)} collective-permute-done((bf16[2,1,4,2048]{3,2,1,0:T(4,128)(2,1)S(1)}, bf16[2,1,4,2048]{3,2,1,0:T(4,128)(2,1)S(1)}, u32[]{:S(2)}, u32[]{:S(2)}) %collective-permute-start) | collective-permute-done | bytes 32800 | tf_op jit(solution)/shard_map/while/body/eval_jaxpr/ppermute | solution.py:13
  221.9 12.0 %collective-permute-done = bf16[2,1,4,2048]{3,2,1,0:T(4,128)(2,1)S(1)} collective-permute-done((bf16[2,1,4,2048]{3,2,1,0:T(4,128)(2,1)S(1)}, bf16[2,1,4,2048]{3,2,1,0:T(4,128)(2,1)S(1)}, u32[]{:S(2)}, u32[]{:S(2)}) %collective-permute-start) | collective-permute-done | bytes 32800 | tf_op jit(solution)/shard_map/while/body/eval_jaxpr/ppermute | solution.py:13
  236.7 12.0 %collective-permute-done = bf16[2,1,4,2048]{3,2,1,0:T(4,128)(2,1)S(1)} collective-permute-done((bf16[2,1,4,2048]{3,2,1,0:T(4,128)(2,1)S(1)}, bf16[2,1,4,2048]{3,2,1,0:T(4,128)(2,1)S(1)}, u32[]{:S(2)}, u32[]{:S(2)}) %collective-permute-start) | collective-permute-done | bytes 32800 | tf_op jit(solution)/shard_map/while/body/eval_jaxpr/ppermute | solution.py:13
  251.4 12.0 %collective-permute-done = bf16[2,1,4,2048]{3,2,1,0:T(4,128)(2,1)S(1)} collective-permute-done((bf16[2,1,4,2048]{3,2,1,0:T(4,128)(2,1)S(1)}, bf16[2,1,4,2048]{3,2,1,0:T(4,128)(2,1)S(1)}, u32[]{:S(2)}, u32[]{:S(2)}) %collective-permute-start) | collective-permute-done | bytes 32800 | tf_op jit(solution)/shard_map/while/body/eval_jaxpr/ppermute | solution.py:13
  266.2 12.0 %collective-permute-done = bf16[2,1,4,2048]{3,2,1,0:T(4,128)(2,1)S(1)} collective-permute-done((bf16[2,1,4,2048]{3,2,1,0:T(4,128)(2,1)S(1)}, bf16[2,1,4,2048]{3,2,1,0:T(4,128)(2,1)S(1)}, u32[]{:S(2)}, u32[]{:S(2)}) %collective-permute-start) | collective-permute-done | bytes 32800 | tf_op jit(solution)/shard_map/while/body/eval_jaxpr/ppermute | solution.py:13
  280.9 12.0 %collective-permute-done = bf16[2,1,4,2048]{3,2,1,0:T(4,128)(2,1)S(1)} collective-permute-done((bf16[2,1,4,2048]{3,2,1,0:T(4,128)(2,1)S(1)}, bf16[2,1,4,2048]{3,2,1,0:T(4,128)(2,1)S(1)}, u32[]{:S(2)}, u32[]{:S(2)}) %collective-permute-start) | collective-permute-done | bytes 32800 | tf_op jit(solution)/shard_map/while/body/eval_jaxpr/ppermute | solution.py:13
  295.7 12.0 %collective-permute-done = bf16[2,1,4,2048]{3,2,1,0:T(4,128)(2,1)S(1)} collective-permute-done((bf16[2,1,4,2048]{3,2,1,0:T(4,128)(2,1)S(1)}, bf16[2,1,4,2048]{3,2,1,0:T(4,128)(2,1)S(1)}, u32[]{:S(2)}, u32[]{:S(2)}) %collective-permute-start) | collective-permute-done | bytes 32800 | tf_op jit(solution)/shard_map/while/body/eval_jaxpr/ppermute | solution.py:13
  310.5 12.0 %collective-permute-done = bf16[2,1,4,2048]{3,2,1,0:T(4,128)(2,1)S(1)} collective-permute-done((bf16[2,1,4,2048]{3,2,1,0:T(4,128)(2,1)S(1)}, bf16[2,1,4,2048]{3,2,1,0:T(4,128)(2,1)S(1)}, u32[]{:S(2)}, u32[]{:S(2)}) %collective-permute-start) | collective-permute-done | bytes 32800 | tf_op jit(solution)/shard_map/while/body/eval_jaxpr/ppermute | solution.py:13
  325.2 12.0 %collective-permute-done = bf16[2,1,4,2048]{3,2,1,0:T(4,128)(2,1)S(1)} collective-permute-done((bf16[2,1,4,2048]{3,2,1,0:T(4,128)(2,1)S(1)}, bf16[2,1,4,2048]{3,2,1,0:T(4,128)(2,1)S(1)}, u32[]{:S(2)}, u32[]{:S(2)}) %collective-permute-start) | collective-permute-done | bytes 32800 | tf_op jit(solution)/shard_map/while/body/eval_jaxpr/ppermute | solution.py:13
  340.0 12.0 %collective-permute-done = bf16[2,1,4,2048]{3,2,1,0:T(4,128)(2,1)S(1)} collective-permute-done((bf16[2,1,4,2048]{3,2,1,0:T(4,128)(2,1)S(1)}, bf16[2,1,4,2048]{3,2,1,0:T(4,128)(2,1)S(1)}, u32[]{:S(2)}, u32[]{:S(2)}) %collective-permute-start) | collective-permute-done | bytes 32800 | tf_op jit(solution)/shard_map/while/body/eval_jaxpr/ppermute | solution.py:13
  354.8 12.0 %collective-permute-done = bf16[2,1,4,2048]{3,2,1,0:T(4,128)(2,1)S(1)} collective-permute-done((bf16[2,1,4,2048]{3,2,1,0:T(4,128)(2,1)S(1)}, bf16[2,1,4,2048]{3,2,1,0:T(4,128)(2,1)S(1)}, u32[]{:S(2)}, u32[]{:S(2)}) %collective-permute-start) | collective-permute-done | bytes 32800 | tf_op jit(solution)/shard_map/while/body/eval_jaxpr/ppermute | solution.py:13
  369.5 12.0 %collective-permute-done = bf16[2,1,4,2048]{3,2,1,0:T(4,128)(2,1)S(1)} collective-permute-done((bf16[2,1,4,2048]{3,2,1,0:T(4,128)(2,1)S(1)}, bf16[2,1,4,2048]{3,2,1,0:T(4,128)(2,1)S(1)}, u32[]{:S(2)}, u32[]{:S(2)}) %collective-permute-start) | collective-permute-done | bytes 32800 | tf_op jit(solution)/shard_map/while/body/eval_jaxpr/ppermute | solution.py:13
  384.3 12.0 %collective-permute-done = bf16[2,1,4,2048]{3,2,1,0:T(4,128)(2,1)S(1)} collective-permute-done((bf16[2,1,4,2048]{3,2,1,0:T(4,128)(2,1)S(1)}, bf16[2,1,4,2048]{3,2,1,0:T(4,128)(2,1)S(1)}, u32[]{:S(2)}, u32[]{:S(2)}) %collective-permute-start) | collective-permute-done | bytes 32800 | tf_op jit(solution)/shard_map/while/body/eval_jaxpr/ppermute | solution.py:13
  399.1 12.0 %collective-permute-done = bf16[2,1,4,2048]{3,2,1,0:T(4,128)(2,1)S(1)} collective-permute-done((bf16[2,1,4,2048]{3,2,1,0:T(4,128)(2,1)S(1)}, bf16[2,1,4,2048]{3,2,1,0:T(4,128)(2,1)S(1)}, u32[]{:S(2)}, u32[]{:S(2)}) %collective-permute-start) | collective-permute-done | bytes 32800 | tf_op jit(solution)/shard_map/while/body/eval_jaxpr/ppermute | solution.py:13
  413.8 12.0 %collective-permute-done = bf16[2,1,4,2048]{3,2,1,0:T(4,128)(2,1)S(1)} collective-permute-done((bf16[2,1,4,2048]{3,2,1,0:T(4,128)(2,1)S(1)}, bf16[2,1,4,2048]{3,2,1,0:T(4,128)(2,1)S(1)}, u32[]{:S(2)}, u32[]{:S(2)}) %collective-permute-start) | collective-permute-done | bytes 32800 | tf_op jit(solution)/shard_map/while/body/eval_jaxpr/ppermute | solution.py:13
  428.6 12.0 %collective-permute-done = bf16[2,1,4,2048]{3,2,1,0:T(4,128)(2,1)S(1)} collective-permute-done((bf16[2,1,4,2048]{3,2,1,0:T(4,128)(2,1)S(1)}, bf16[2,1,4,2048]{3,2,1,0:T(4,128)(2,1)S(1)}, u32[]{:S(2)}, u32[]{:S(2)}) %collective-permute-start) | collective-permute-done | bytes 32800 | tf_op jit(solution)/shard_map/while/body/eval_jaxpr/ppermute | solution.py:13
  443.3 12.0 %collective-permute-done = bf16[2,1,4,2048]{3,2,1,0:T(4,128)(2,1)S(1)} collective-permute-done((bf16[2,1,4,2048]{3,2,1,0:T(4,128)(2,1)S(1)}, bf16[2,1,4,2048]{3,2,1,0:T(4,128)(2,1)S(1)}, u32[]{:S(2)}, u32[]{:S(2)}) %collective-permute-start) | collective-permute-done | bytes 32800 | tf_op jit(solution)/shard_map/while/body/eval_jaxpr/ppermute | solution.py:13
  458.1 12.0 %collective-permute-done = bf16[2,1,4,2048]{3,2,1,0:T(4,128)(2,1)S(1)} collective-permute-done((bf16[2,1,4,2048]{3,2,1,0:T(4,128)(2,1)S(1)}, bf16[2,1,4,2048]{3,2,1,0:T(4,128)(2,1)S(1)}, u32[]{:S(2)}, u32[]{:S(2)}) %collective-permute-start) | collective-permute-done | bytes 32800 | tf_op jit(solution)/shard_map/while/body/eval_jaxpr/ppermute | solution.py:13
  664.8 12.0 %collective-permute-done = bf16[2,1,4,2048]{3,2,1,0:T(4,128)(2,1)S(1)} collective-permute-done((bf16[2,1,4,2048]{3,2,1,0:T(4,128)(2,1)S(1)}, bf16[2,1,4,2048]{3,2,1,0:T(4,128)(2,1)S(1)}, u32[]{:S(2)}, u32[]{:S(2)}) %collective-permute-start) | collective-permute-done | bytes 32800 | tf_op jit(solution)/shard_map/while/body/eval_jaxpr/ppermute | solution.py:13
  694.4 12.0 %collective-permute-done = bf16[2,1,4,2048]{3,2,1,0:T(4,128)(2,1)S(1)} collective-permute-done((bf16[2,1,4,2048]{3,2,1,0:T(4,128)(2,1)S(1)}, bf16[2,1,4,2048]{3,2,1,0:T(4,128)(2,1)S(1)}, u32[]{:S(2)}, u32[]{:S(2)}) %collective-permute-start) | collective-permute-done | bytes 32800 | tf_op jit(solution)/shard_map/while/body/eval_jaxpr/ppermute | solution.py:13
  709.1 12.1 %collective-permute-done = bf16[2,1,4,2048]{3,2,1,0:T(4,128)(2,1)S(1)} collective-permute-done((bf16[2,1,4,2048]{3,2,1,0:T(4,128)(2,1)S(1)}, bf16[2,1,4,2048]{3,2,1,0:T(4,128)(2,1)S(1)}, u32[]{:S(2)}, u32[]{:S(2)}) %collective-permute-start) | collective-permute-done | bytes 32800 | tf_op jit(solution)/shard_map/while/body/eval_jaxpr/ppermute | solution.py:13
  724.0 14.1 %collective-permute-done = bf16[2,1,4,2048]{3,2,1,0:T(4,128)(2,1)S(1)} collective-permute-done((bf16[2,1,4,2048]{3,2,1,0:T(4,128)(2,1)S(1)}, bf16[2,1,4,2048]{3,2,1,0:T(4,128)(2,1)S(1)}, u32[]{:S(2)}, u32[]{:S(2)}) %collective-permute-start) | collective-permute-done | bytes 32800 | tf_op jit(solution)/shard_map/while/body/eval_jaxpr/ppermute | solution.py:13
  740.9 12.3 %collective-permute-done = bf16[2,1,4,2048]{3,2,1,0:T(4,128)(2,1)S(1)} collective-permute-done((bf16[2,1,4,2048]{3,2,1,0:T(4,128)(2,1)S(1)}, bf16[2,1,4,2048]{3,2,1,0:T(4,128)(2,1)S(1)}, u32[]{:S(2)}, u32[]{:S(2)}) %collective-permute-start) | collective-permute-done | bytes 32800 | tf_op jit(solution)/shard_map/while/body/eval_jaxpr/ppermute | solution.py:13
  756.0 13.9 %collective-permute-done = bf16[2,1,4,2048]{3,2,1,0:T(4,128)(2,1)S(1)} collective-permute-done((bf16[2,1,4,2048]{3,2,1,0:T(4,128)(2,1)S(1)}, bf16[2,1,4,2048]{3,2,1,0:T(4,128)(2,1)S(1)}, u32[]{:S(2)}, u32[]{:S(2)}) %collective-permute-start) | collective-permute-done | bytes 32800 | tf_op jit(solution)/shard_map/while/body/eval_jaxpr/ppermute | solution.py:13
  787.4 12.0 %collective-permute-done = bf16[2,1,4,2048]{3,2,1,0:T(4,128)(2,1)S(1)} collective-permute-done((bf16[2,1,4,2048]{3,2,1,0:T(4,128)(2,1)S(1)}, bf16[2,1,4,2048]{3,2,1,0:T(4,128)(2,1)S(1)}, u32[]{:S(2)}, u32[]{:S(2)}) %collective-permute-start) | collective-permute-done | bytes 32800 | tf_op jit(solution)/shard_map/while/body/eval_jaxpr/ppermute | solution.py:13
  816.9 12.1 %collective-permute-done = bf16[2,1,4,2048]{3,2,1,0:T(4,128)(2,1)S(1)} collective-permute-done((bf16[2,1,4,2048]{3,2,1,0:T(4,128)(2,1)S(1)}, bf16[2,1,4,2048]{3,2,1,0:T(4,128)(2,1)S(1)}, u32[]{:S(2)}, u32[]{:S(2)}) %collective-permute-start) | collective-permute-done | bytes 32800 | tf_op jit(solution)/shard_map/while/body/eval_jaxpr/ppermute | solution.py:13
  831.8 16.4 %collective-permute-done = bf16[2,1,4,2048]{3,2,1,0:T(4,128)(2,1)S(1)} collective-permute-done((bf16[2,1,4,2048]{3,2,1,0:T(4,128)(2,1)S(1)}, bf16[2,1,4,2048]{3,2,1,0:T(4,128)(2,1)S(1)}, u32[]{:S(2)}, u32[]{:S(2)}) %collective-permute-start) | collective-permute-done | bytes 32800 | tf_op jit(solution)/shard_map/while/body/eval_jaxpr/ppermute | solution.py:13
  851.0 12.2 %collective-permute-done = bf16[2,1,4,2048]{3,2,1,0:T(4,128)(2,1)S(1)} collective-permute-done((bf16[2,1,4,2048]{3,2,1,0:T(4,128)(2,1)S(1)}, bf16[2,1,4,2048]{3,2,1,0:T(4,128)(2,1)S(1)}, u32[]{:S(2)}, u32[]{:S(2)}) %collective-permute-start) | collective-permute-done | bytes 32800 | tf_op jit(solution)/shard_map/while/body/eval_jaxpr/ppermute | solution.py:13
  866.0 12.8 %collective-permute-done = bf16[2,1,4,2048]{3,2,1,0:T(4,128)(2,1)S(1)} collective-permute-done((bf16[2,1,4,2048]{3,2,1,0:T(4,128)(2,1)S(1)}, bf16[2,1,4,2048]{3,2,1,0:T(4,128)(2,1)S(1)}, u32[]{:S(2)}, u32[]{:S(2)}) %collective-permute-start) | collective-permute-done | bytes 32800 | tf_op jit(solution)/shard_map/while/body/eval_jaxpr/ppermute | solution.py:13
  881.6 12.6 %collective-permute-done = bf16[2,1,4,2048]{3,2,1,0:T(4,128)(2,1)S(1)} collective-permute-done((bf16[2,1,4,2048]{3,2,1,0:T(4,128)(2,1)S(1)}, bf16[2,1,4,2048]{3,2,1,0:T(4,128)(2,1)S(1)}, u32[]{:S(2)}, u32[]{:S(2)}) %collective-permute-start) | collective-permute-done | bytes 32800 | tf_op jit(solution)/shard_map/while/body/eval_jaxpr/ppermute | solution.py:13
  911.7 12.2 %collective-permute-done = bf16[2,1,4,2048]{3,2,1,0:T(4,128)(2,1)S(1)} collective-permute-done((bf16[2,1,4,2048]{3,2,1,0:T(4,128)(2,1)S(1)}, bf16[2,1,4,2048]{3,2,1,0:T(4,128)(2,1)S(1)}, u32[]{:S(2)}, u32[]{:S(2)}) %collective-permute-start) | collective-permute-done | bytes 32800 | tf_op jit(solution)/shard_map/while/body/eval_jaxpr/ppermute | solution.py:13
  926.7 14.2 %collective-permute-done = bf16[2,1,4,2048]{3,2,1,0:T(4,128)(2,1)S(1)} collective-permute-done((bf16[2,1,4,2048]{3,2,1,0:T(4,128)(2,1)S(1)}, bf16[2,1,4,2048]{3,2,1,0:T(4,128)(2,1)S(1)}, u32[]{:S(2)}, u32[]{:S(2)}) %collective-permute-start) | collective-permute-done | bytes 32800 | tf_op jit(solution)/shard_map/while/body/eval_jaxpr/ppermute | solution.py:13
  964.9 12.9 %fusion.14 = f32[4,64,4,256]{3,1,2,0:T(8,128)S(1)} fusion(f32[2048,256]{1,0:T(8,128)S(1)} %get-tuple-element.160, f32[2048,256]{1,0:T(8,128)S(1)} %get-tuple-element.159, bf16[4,64,4,4096]{3,2,1,0:T(4,128)(2,1)} %get-tuple-element.138, f32[64]{0:T(128)S(1)} %convert_bitcast_fusion.6), kind=kOutput, calls=%fused_computation.27 | convolution fusion | flops 2150891520 | bytes 13631744 | tf_op jit(solution)/shard_map/dot_general | solution.py:51
  978.5 146.2 %all-reduce.2 = bf16[4,256,256]{2,0,1:T(4,128)(2,1)S(1)} all-reduce(f32[4,256,256]{2,0,1:T(4,128)S(1)} %bitcast.81), channel_id=2, replica_groups=mesh['sta'=64,'win'=8] {'win'}, use_global_device_ids=true, to_apply=%region_3.4.clone | all-reduce | flops 262144 | bytes 1572864
  (414 shorter events, 408.6 us)
Async XLA Ops:
  10.7 16.4 %collective-permute-start = (bf16[2,1,4,2048]{3,2,1,0:T(4,128)(2,1)S(1)}, bf16[2,1,4,2048]{3,2,1,0:T(4,128)(2,1)S(1)}, u32[]{:S(2)}, u32[]{:S(2)}) collective-permute-start(bf16[2,1,4,2048]{3,2,1,0:T(4,128)(2,1)S(1)} %get-tuple-element.215), channel_id=1, source_target_pairs={{0,8},{8,16},{16,24},{24,32},{32,40},{40,48},{48,56},{56,64},{64,7... | collective-permute-start | bytes 98312 | tf_op jit(solution)/shard_map/while/body/eval_jaxpr/ppermute | solution.py:13
  28.0 13.9 %collective-permute-start = (bf16[2,1,4,2048]{3,2,1,0:T(4,128)(2,1)S(1)}, bf16[2,1,4,2048]{3,2,1,0:T(4,128)(2,1)S(1)}, u32[]{:S(2)}, u32[]{:S(2)}) collective-permute-start(bf16[2,1,4,2048]{3,2,1,0:T(4,128)(2,1)S(1)} %get-tuple-element.215), channel_id=1, source_target_pairs={{0,8},{8,16},{16,24},{24,32},{32,40},{40,48},{48,56},{56,64},{64,7... | collective-permute-start | bytes 98312 | tf_op jit(solution)/shard_map/while/body/eval_jaxpr/ppermute | solution.py:13
  42.7 13.9 %collective-permute-start = (bf16[2,1,4,2048]{3,2,1,0:T(4,128)(2,1)S(1)}, bf16[2,1,4,2048]{3,2,1,0:T(4,128)(2,1)S(1)}, u32[]{:S(2)}, u32[]{:S(2)}) collective-permute-start(bf16[2,1,4,2048]{3,2,1,0:T(4,128)(2,1)S(1)} %get-tuple-element.215), channel_id=1, source_target_pairs={{0,8},{8,16},{16,24},{24,32},{32,40},{40,48},{48,56},{56,64},{64,7... | collective-permute-start | bytes 98312 | tf_op jit(solution)/shard_map/while/body/eval_jaxpr/ppermute | solution.py:13
  57.5 13.9 %collective-permute-start = (bf16[2,1,4,2048]{3,2,1,0:T(4,128)(2,1)S(1)}, bf16[2,1,4,2048]{3,2,1,0:T(4,128)(2,1)S(1)}, u32[]{:S(2)}, u32[]{:S(2)}) collective-permute-start(bf16[2,1,4,2048]{3,2,1,0:T(4,128)(2,1)S(1)} %get-tuple-element.215), channel_id=1, source_target_pairs={{0,8},{8,16},{16,24},{24,32},{32,40},{40,48},{48,56},{56,64},{64,7... | collective-permute-start | bytes 98312 | tf_op jit(solution)/shard_map/while/body/eval_jaxpr/ppermute | solution.py:13
  72.3 13.9 %collective-permute-start = (bf16[2,1,4,2048]{3,2,1,0:T(4,128)(2,1)S(1)}, bf16[2,1,4,2048]{3,2,1,0:T(4,128)(2,1)S(1)}, u32[]{:S(2)}, u32[]{:S(2)}) collective-permute-start(bf16[2,1,4,2048]{3,2,1,0:T(4,128)(2,1)S(1)} %get-tuple-element.215), channel_id=1, source_target_pairs={{0,8},{8,16},{16,24},{24,32},{32,40},{40,48},{48,56},{56,64},{64,7... | collective-permute-start | bytes 98312 | tf_op jit(solution)/shard_map/while/body/eval_jaxpr/ppermute | solution.py:13
  87.0 13.9 %collective-permute-start = (bf16[2,1,4,2048]{3,2,1,0:T(4,128)(2,1)S(1)}, bf16[2,1,4,2048]{3,2,1,0:T(4,128)(2,1)S(1)}, u32[]{:S(2)}, u32[]{:S(2)}) collective-permute-start(bf16[2,1,4,2048]{3,2,1,0:T(4,128)(2,1)S(1)} %get-tuple-element.215), channel_id=1, source_target_pairs={{0,8},{8,16},{16,24},{24,32},{32,40},{40,48},{48,56},{56,64},{64,7... | collective-permute-start | bytes 98312 | tf_op jit(solution)/shard_map/while/body/eval_jaxpr/ppermute | solution.py:13
  101.8 13.9 %collective-permute-start = (bf16[2,1,4,2048]{3,2,1,0:T(4,128)(2,1)S(1)}, bf16[2,1,4,2048]{3,2,1,0:T(4,128)(2,1)S(1)}, u32[]{:S(2)}, u32[]{:S(2)}) collective-permute-start(bf16[2,1,4,2048]{3,2,1,0:T(4,128)(2,1)S(1)} %get-tuple-element.215), channel_id=1, source_target_pairs={{0,8},{8,16},{16,24},{24,32},{32,40},{40,48},{48,56},{56,64},{64,7... | collective-permute-start | bytes 98312 | tf_op jit(solution)/shard_map/while/body/eval_jaxpr/ppermute | solution.py:13
  116.6 13.9 %collective-permute-start = (bf16[2,1,4,2048]{3,2,1,0:T(4,128)(2,1)S(1)}, bf16[2,1,4,2048]{3,2,1,0:T(4,128)(2,1)S(1)}, u32[]{:S(2)}, u32[]{:S(2)}) collective-permute-start(bf16[2,1,4,2048]{3,2,1,0:T(4,128)(2,1)S(1)} %get-tuple-element.215), channel_id=1, source_target_pairs={{0,8},{8,16},{16,24},{24,32},{32,40},{40,48},{48,56},{56,64},{64,7... | collective-permute-start | bytes 98312 | tf_op jit(solution)/shard_map/while/body/eval_jaxpr/ppermute | solution.py:13
  131.3 13.9 %collective-permute-start = (bf16[2,1,4,2048]{3,2,1,0:T(4,128)(2,1)S(1)}, bf16[2,1,4,2048]{3,2,1,0:T(4,128)(2,1)S(1)}, u32[]{:S(2)}, u32[]{:S(2)}) collective-permute-start(bf16[2,1,4,2048]{3,2,1,0:T(4,128)(2,1)S(1)} %get-tuple-element.215), channel_id=1, source_target_pairs={{0,8},{8,16},{16,24},{24,32},{32,40},{40,48},{48,56},{56,64},{64,7... | collective-permute-start | bytes 98312 | tf_op jit(solution)/shard_map/while/body/eval_jaxpr/ppermute | solution.py:13
  146.1 13.9 %collective-permute-start = (bf16[2,1,4,2048]{3,2,1,0:T(4,128)(2,1)S(1)}, bf16[2,1,4,2048]{3,2,1,0:T(4,128)(2,1)S(1)}, u32[]{:S(2)}, u32[]{:S(2)}) collective-permute-start(bf16[2,1,4,2048]{3,2,1,0:T(4,128)(2,1)S(1)} %get-tuple-element.215), channel_id=1, source_target_pairs={{0,8},{8,16},{16,24},{24,32},{32,40},{40,48},{48,56},{56,64},{64,7... | collective-permute-start | bytes 98312 | tf_op jit(solution)/shard_map/while/body/eval_jaxpr/ppermute | solution.py:13
  160.9 13.9 %collective-permute-start = (bf16[2,1,4,2048]{3,2,1,0:T(4,128)(2,1)S(1)}, bf16[2,1,4,2048]{3,2,1,0:T(4,128)(2,1)S(1)}, u32[]{:S(2)}, u32[]{:S(2)}) collective-permute-start(bf16[2,1,4,2048]{3,2,1,0:T(4,128)(2,1)S(1)} %get-tuple-element.215), channel_id=1, source_target_pairs={{0,8},{8,16},{16,24},{24,32},{32,40},{40,48},{48,56},{56,64},{64,7... | collective-permute-start | bytes 98312 | tf_op jit(solution)/shard_map/while/body/eval_jaxpr/ppermute | solution.py:13
  175.6 13.9 %collective-permute-start = (bf16[2,1,4,2048]{3,2,1,0:T(4,128)(2,1)S(1)}, bf16[2,1,4,2048]{3,2,1,0:T(4,128)(2,1)S(1)}, u32[]{:S(2)}, u32[]{:S(2)}) collective-permute-start(bf16[2,1,4,2048]{3,2,1,0:T(4,128)(2,1)S(1)} %get-tuple-element.215), channel_id=1, source_target_pairs={{0,8},{8,16},{16,24},{24,32},{32,40},{40,48},{48,56},{56,64},{64,7... | collective-permute-start | bytes 98312 | tf_op jit(solution)/shard_map/while/body/eval_jaxpr/ppermute | solution.py:13
  190.4 13.9 %collective-permute-start = (bf16[2,1,4,2048]{3,2,1,0:T(4,128)(2,1)S(1)}, bf16[2,1,4,2048]{3,2,1,0:T(4,128)(2,1)S(1)}, u32[]{:S(2)}, u32[]{:S(2)}) collective-permute-start(bf16[2,1,4,2048]{3,2,1,0:T(4,128)(2,1)S(1)} %get-tuple-element.215), channel_id=1, source_target_pairs={{0,8},{8,16},{16,24},{24,32},{32,40},{40,48},{48,56},{56,64},{64,7... | collective-permute-start | bytes 98312 | tf_op jit(solution)/shard_map/while/body/eval_jaxpr/ppermute | solution.py:13
  205.2 13.9 %collective-permute-start = (bf16[2,1,4,2048]{3,2,1,0:T(4,128)(2,1)S(1)}, bf16[2,1,4,2048]{3,2,1,0:T(4,128)(2,1)S(1)}, u32[]{:S(2)}, u32[]{:S(2)}) collective-permute-start(bf16[2,1,4,2048]{3,2,1,0:T(4,128)(2,1)S(1)} %get-tuple-element.215), channel_id=1, source_target_pairs={{0,8},{8,16},{16,24},{24,32},{32,40},{40,48},{48,56},{56,64},{64,7... | collective-permute-start | bytes 98312 | tf_op jit(solution)/shard_map/while/body/eval_jaxpr/ppermute | solution.py:13
  219.9 13.9 %collective-permute-start = (bf16[2,1,4,2048]{3,2,1,0:T(4,128)(2,1)S(1)}, bf16[2,1,4,2048]{3,2,1,0:T(4,128)(2,1)S(1)}, u32[]{:S(2)}, u32[]{:S(2)}) collective-permute-start(bf16[2,1,4,2048]{3,2,1,0:T(4,128)(2,1)S(1)} %get-tuple-element.215), channel_id=1, source_target_pairs={{0,8},{8,16},{16,24},{24,32},{32,40},{40,48},{48,56},{56,64},{64,7... | collective-permute-start | bytes 98312 | tf_op jit(solution)/shard_map/while/body/eval_jaxpr/ppermute | solution.py:13
  234.7 13.9 %collective-permute-start = (bf16[2,1,4,2048]{3,2,1,0:T(4,128)(2,1)S(1)}, bf16[2,1,4,2048]{3,2,1,0:T(4,128)(2,1)S(1)}, u32[]{:S(2)}, u32[]{:S(2)}) collective-permute-start(bf16[2,1,4,2048]{3,2,1,0:T(4,128)(2,1)S(1)} %get-tuple-element.215), channel_id=1, source_target_pairs={{0,8},{8,16},{16,24},{24,32},{32,40},{40,48},{48,56},{56,64},{64,7... | collective-permute-start | bytes 98312 | tf_op jit(solution)/shard_map/while/body/eval_jaxpr/ppermute | solution.py:13
  249.4 13.9 %collective-permute-start = (bf16[2,1,4,2048]{3,2,1,0:T(4,128)(2,1)S(1)}, bf16[2,1,4,2048]{3,2,1,0:T(4,128)(2,1)S(1)}, u32[]{:S(2)}, u32[]{:S(2)}) collective-permute-start(bf16[2,1,4,2048]{3,2,1,0:T(4,128)(2,1)S(1)} %get-tuple-element.215), channel_id=1, source_target_pairs={{0,8},{8,16},{16,24},{24,32},{32,40},{40,48},{48,56},{56,64},{64,7... | collective-permute-start | bytes 98312 | tf_op jit(solution)/shard_map/while/body/eval_jaxpr/ppermute | solution.py:13
  264.2 13.9 %collective-permute-start = (bf16[2,1,4,2048]{3,2,1,0:T(4,128)(2,1)S(1)}, bf16[2,1,4,2048]{3,2,1,0:T(4,128)(2,1)S(1)}, u32[]{:S(2)}, u32[]{:S(2)}) collective-permute-start(bf16[2,1,4,2048]{3,2,1,0:T(4,128)(2,1)S(1)} %get-tuple-element.215), channel_id=1, source_target_pairs={{0,8},{8,16},{16,24},{24,32},{32,40},{40,48},{48,56},{56,64},{64,7... | collective-permute-start | bytes 98312 | tf_op jit(solution)/shard_map/while/body/eval_jaxpr/ppermute | solution.py:13
  279.0 13.9 %collective-permute-start = (bf16[2,1,4,2048]{3,2,1,0:T(4,128)(2,1)S(1)}, bf16[2,1,4,2048]{3,2,1,0:T(4,128)(2,1)S(1)}, u32[]{:S(2)}, u32[]{:S(2)}) collective-permute-start(bf16[2,1,4,2048]{3,2,1,0:T(4,128)(2,1)S(1)} %get-tuple-element.215), channel_id=1, source_target_pairs={{0,8},{8,16},{16,24},{24,32},{32,40},{40,48},{48,56},{56,64},{64,7... | collective-permute-start | bytes 98312 | tf_op jit(solution)/shard_map/while/body/eval_jaxpr/ppermute | solution.py:13
  293.7 13.9 %collective-permute-start = (bf16[2,1,4,2048]{3,2,1,0:T(4,128)(2,1)S(1)}, bf16[2,1,4,2048]{3,2,1,0:T(4,128)(2,1)S(1)}, u32[]{:S(2)}, u32[]{:S(2)}) collective-permute-start(bf16[2,1,4,2048]{3,2,1,0:T(4,128)(2,1)S(1)} %get-tuple-element.215), channel_id=1, source_target_pairs={{0,8},{8,16},{16,24},{24,32},{32,40},{40,48},{48,56},{56,64},{64,7... | collective-permute-start | bytes 98312 | tf_op jit(solution)/shard_map/while/body/eval_jaxpr/ppermute | solution.py:13
  308.5 13.9 %collective-permute-start = (bf16[2,1,4,2048]{3,2,1,0:T(4,128)(2,1)S(1)}, bf16[2,1,4,2048]{3,2,1,0:T(4,128)(2,1)S(1)}, u32[]{:S(2)}, u32[]{:S(2)}) collective-permute-start(bf16[2,1,4,2048]{3,2,1,0:T(4,128)(2,1)S(1)} %get-tuple-element.215), channel_id=1, source_target_pairs={{0,8},{8,16},{16,24},{24,32},{32,40},{40,48},{48,56},{56,64},{64,7... | collective-permute-start | bytes 98312 | tf_op jit(solution)/shard_map/while/body/eval_jaxpr/ppermute | solution.py:13
  323.3 13.9 %collective-permute-start = (bf16[2,1,4,2048]{3,2,1,0:T(4,128)(2,1)S(1)}, bf16[2,1,4,2048]{3,2,1,0:T(4,128)(2,1)S(1)}, u32[]{:S(2)}, u32[]{:S(2)}) collective-permute-start(bf16[2,1,4,2048]{3,2,1,0:T(4,128)(2,1)S(1)} %get-tuple-element.215), channel_id=1, source_target_pairs={{0,8},{8,16},{16,24},{24,32},{32,40},{40,48},{48,56},{56,64},{64,7... | collective-permute-start | bytes 98312 | tf_op jit(solution)/shard_map/while/body/eval_jaxpr/ppermute | solution.py:13
  352.8 13.9 %collective-permute-start = (bf16[2,1,4,2048]{3,2,1,0:T(4,128)(2,1)S(1)}, bf16[2,1,4,2048]{3,2,1,0:T(4,128)(2,1)S(1)}, u32[]{:S(2)}, u32[]{:S(2)}) collective-permute-start(bf16[2,1,4,2048]{3,2,1,0:T(4,128)(2,1)S(1)} %get-tuple-element.215), channel_id=1, source_target_pairs={{0,8},{8,16},{16,24},{24,32},{32,40},{40,48},{48,56},{56,64},{64,7... | collective-permute-start | bytes 98312 | tf_op jit(solution)/shard_map/while/body/eval_jaxpr/ppermute | solution.py:13
  367.5 13.9 %collective-permute-start = (bf16[2,1,4,2048]{3,2,1,0:T(4,128)(2,1)S(1)}, bf16[2,1,4,2048]{3,2,1,0:T(4,128)(2,1)S(1)}, u32[]{:S(2)}, u32[]{:S(2)}) collective-permute-start(bf16[2,1,4,2048]{3,2,1,0:T(4,128)(2,1)S(1)} %get-tuple-element.215), channel_id=1, source_target_pairs={{0,8},{8,16},{16,24},{24,32},{32,40},{40,48},{48,56},{56,64},{64,7... | collective-permute-start | bytes 98312 | tf_op jit(solution)/shard_map/while/body/eval_jaxpr/ppermute | solution.py:13
  411.8 13.9 %collective-permute-start = (bf16[2,1,4,2048]{3,2,1,0:T(4,128)(2,1)S(1)}, bf16[2,1,4,2048]{3,2,1,0:T(4,128)(2,1)S(1)}, u32[]{:S(2)}, u32[]{:S(2)}) collective-permute-start(bf16[2,1,4,2048]{3,2,1,0:T(4,128)(2,1)S(1)} %get-tuple-element.215), channel_id=1, source_target_pairs={{0,8},{8,16},{16,24},{24,32},{32,40},{40,48},{48,56},{56,64},{64,7... | collective-permute-start | bytes 98312 | tf_op jit(solution)/shard_map/while/body/eval_jaxpr/ppermute | solution.py:13
  426.6 13.9 %collective-permute-start = (bf16[2,1,4,2048]{3,2,1,0:T(4,128)(2,1)S(1)}, bf16[2,1,4,2048]{3,2,1,0:T(4,128)(2,1)S(1)}, u32[]{:S(2)}, u32[]{:S(2)}) collective-permute-start(bf16[2,1,4,2048]{3,2,1,0:T(4,128)(2,1)S(1)} %get-tuple-element.215), channel_id=1, source_target_pairs={{0,8},{8,16},{16,24},{24,32},{32,40},{40,48},{48,56},{56,64},{64,7... | collective-permute-start | bytes 98312 | tf_op jit(solution)/shard_map/while/body/eval_jaxpr/ppermute | solution.py:13
  456.1 13.9 %collective-permute-start = (bf16[2,1,4,2048]{3,2,1,0:T(4,128)(2,1)S(1)}, bf16[2,1,4,2048]{3,2,1,0:T(4,128)(2,1)S(1)}, u32[]{:S(2)}, u32[]{:S(2)}) collective-permute-start(bf16[2,1,4,2048]{3,2,1,0:T(4,128)(2,1)S(1)} %get-tuple-element.215), channel_id=1, source_target_pairs={{0,8},{8,16},{16,24},{24,32},{32,40},{40,48},{48,56},{56,64},{64,7... | collective-permute-start | bytes 98312 | tf_op jit(solution)/shard_map/while/body/eval_jaxpr/ppermute | solution.py:13
  515.2 13.9 %collective-permute-start = (bf16[2,1,4,2048]{3,2,1,0:T(4,128)(2,1)S(1)}, bf16[2,1,4,2048]{3,2,1,0:T(4,128)(2,1)S(1)}, u32[]{:S(2)}, u32[]{:S(2)}) collective-permute-start(bf16[2,1,4,2048]{3,2,1,0:T(4,128)(2,1)S(1)} %get-tuple-element.215), channel_id=1, source_target_pairs={{0,8},{8,16},{16,24},{24,32},{32,40},{40,48},{48,56},{56,64},{64,7... | collective-permute-start | bytes 98312 | tf_op jit(solution)/shard_map/while/body/eval_jaxpr/ppermute | solution.py:13
  544.7 13.9 %collective-permute-start = (bf16[2,1,4,2048]{3,2,1,0:T(4,128)(2,1)S(1)}, bf16[2,1,4,2048]{3,2,1,0:T(4,128)(2,1)S(1)}, u32[]{:S(2)}, u32[]{:S(2)}) collective-permute-start(bf16[2,1,4,2048]{3,2,1,0:T(4,128)(2,1)S(1)} %get-tuple-element.215), channel_id=1, source_target_pairs={{0,8},{8,16},{16,24},{24,32},{32,40},{40,48},{48,56},{56,64},{64,7... | collective-permute-start | bytes 98312 | tf_op jit(solution)/shard_map/while/body/eval_jaxpr/ppermute | solution.py:13
  589.0 13.9 %collective-permute-start = (bf16[2,1,4,2048]{3,2,1,0:T(4,128)(2,1)S(1)}, bf16[2,1,4,2048]{3,2,1,0:T(4,128)(2,1)S(1)}, u32[]{:S(2)}, u32[]{:S(2)}) collective-permute-start(bf16[2,1,4,2048]{3,2,1,0:T(4,128)(2,1)S(1)} %get-tuple-element.215), channel_id=1, source_target_pairs={{0,8},{8,16},{16,24},{24,32},{32,40},{40,48},{48,56},{56,64},{64,7... | collective-permute-start | bytes 98312 | tf_op jit(solution)/shard_map/while/body/eval_jaxpr/ppermute | solution.py:13
  603.8 13.9 %collective-permute-start = (bf16[2,1,4,2048]{3,2,1,0:T(4,128)(2,1)S(1)}, bf16[2,1,4,2048]{3,2,1,0:T(4,128)(2,1)S(1)}, u32[]{:S(2)}, u32[]{:S(2)}) collective-permute-start(bf16[2,1,4,2048]{3,2,1,0:T(4,128)(2,1)S(1)} %get-tuple-element.215), channel_id=1, source_target_pairs={{0,8},{8,16},{16,24},{24,32},{32,40},{40,48},{48,56},{56,64},{64,7... | collective-permute-start | bytes 98312 | tf_op jit(solution)/shard_map/while/body/eval_jaxpr/ppermute | solution.py:13
  618.5 13.9 %collective-permute-start = (bf16[2,1,4,2048]{3,2,1,0:T(4,128)(2,1)S(1)}, bf16[2,1,4,2048]{3,2,1,0:T(4,128)(2,1)S(1)}, u32[]{:S(2)}, u32[]{:S(2)}) collective-permute-start(bf16[2,1,4,2048]{3,2,1,0:T(4,128)(2,1)S(1)} %get-tuple-element.215), channel_id=1, source_target_pairs={{0,8},{8,16},{16,24},{24,32},{32,40},{40,48},{48,56},{56,64},{64,7... | collective-permute-start | bytes 98312 | tf_op jit(solution)/shard_map/while/body/eval_jaxpr/ppermute | solution.py:13
  648.1 13.9 %collective-permute-start = (bf16[2,1,4,2048]{3,2,1,0:T(4,128)(2,1)S(1)}, bf16[2,1,4,2048]{3,2,1,0:T(4,128)(2,1)S(1)}, u32[]{:S(2)}, u32[]{:S(2)}) collective-permute-start(bf16[2,1,4,2048]{3,2,1,0:T(4,128)(2,1)S(1)} %get-tuple-element.215), channel_id=1, source_target_pairs={{0,8},{8,16},{16,24},{24,32},{32,40},{40,48},{48,56},{56,64},{64,7... | collective-permute-start | bytes 98312 | tf_op jit(solution)/shard_map/while/body/eval_jaxpr/ppermute | solution.py:13
  662.8 14.0 %collective-permute-start = (bf16[2,1,4,2048]{3,2,1,0:T(4,128)(2,1)S(1)}, bf16[2,1,4,2048]{3,2,1,0:T(4,128)(2,1)S(1)}, u32[]{:S(2)}, u32[]{:S(2)}) collective-permute-start(bf16[2,1,4,2048]{3,2,1,0:T(4,128)(2,1)S(1)} %get-tuple-element.215), channel_id=1, source_target_pairs={{0,8},{8,16},{16,24},{24,32},{32,40},{40,48},{48,56},{56,64},{64,7... | collective-permute-start | bytes 98312 | tf_op jit(solution)/shard_map/while/body/eval_jaxpr/ppermute | solution.py:13
  692.4 13.9 %collective-permute-start = (bf16[2,1,4,2048]{3,2,1,0:T(4,128)(2,1)S(1)}, bf16[2,1,4,2048]{3,2,1,0:T(4,128)(2,1)S(1)}, u32[]{:S(2)}, u32[]{:S(2)}) collective-permute-start(bf16[2,1,4,2048]{3,2,1,0:T(4,128)(2,1)S(1)} %get-tuple-element.215), channel_id=1, source_target_pairs={{0,8},{8,16},{16,24},{24,32},{32,40},{40,48},{48,56},{56,64},{64,7... | collective-permute-start | bytes 98312 | tf_op jit(solution)/shard_map/while/body/eval_jaxpr/ppermute | solution.py:13
  707.2 14.0 %collective-permute-start = (bf16[2,1,4,2048]{3,2,1,0:T(4,128)(2,1)S(1)}, bf16[2,1,4,2048]{3,2,1,0:T(4,128)(2,1)S(1)}, u32[]{:S(2)}, u32[]{:S(2)}) collective-permute-start(bf16[2,1,4,2048]{3,2,1,0:T(4,128)(2,1)S(1)} %get-tuple-element.215), channel_id=1, source_target_pairs={{0,8},{8,16},{16,24},{24,32},{32,40},{40,48},{48,56},{56,64},{64,7... | collective-permute-start | bytes 98312 | tf_op jit(solution)/shard_map/while/body/eval_jaxpr/ppermute | solution.py:13
  722.0 16.1 %collective-permute-start = (bf16[2,1,4,2048]{3,2,1,0:T(4,128)(2,1)S(1)}, bf16[2,1,4,2048]{3,2,1,0:T(4,128)(2,1)S(1)}, u32[]{:S(2)}, u32[]{:S(2)}) collective-permute-start(bf16[2,1,4,2048]{3,2,1,0:T(4,128)(2,1)S(1)} %get-tuple-element.215), channel_id=1, source_target_pairs={{0,8},{8,16},{16,24},{24,32},{32,40},{40,48},{48,56},{56,64},{64,7... | collective-permute-start | bytes 98312 | tf_op jit(solution)/shard_map/while/body/eval_jaxpr/ppermute | solution.py:13
  738.9 14.3 %collective-permute-start = (bf16[2,1,4,2048]{3,2,1,0:T(4,128)(2,1)S(1)}, bf16[2,1,4,2048]{3,2,1,0:T(4,128)(2,1)S(1)}, u32[]{:S(2)}, u32[]{:S(2)}) collective-permute-start(bf16[2,1,4,2048]{3,2,1,0:T(4,128)(2,1)S(1)} %get-tuple-element.215), channel_id=1, source_target_pairs={{0,8},{8,16},{16,24},{24,32},{32,40},{40,48},{48,56},{56,64},{64,7... | collective-permute-start | bytes 98312 | tf_op jit(solution)/shard_map/while/body/eval_jaxpr/ppermute | solution.py:13
  754.0 15.8 %collective-permute-start = (bf16[2,1,4,2048]{3,2,1,0:T(4,128)(2,1)S(1)}, bf16[2,1,4,2048]{3,2,1,0:T(4,128)(2,1)S(1)}, u32[]{:S(2)}, u32[]{:S(2)}) collective-permute-start(bf16[2,1,4,2048]{3,2,1,0:T(4,128)(2,1)S(1)} %get-tuple-element.215), channel_id=1, source_target_pairs={{0,8},{8,16},{16,24},{24,32},{32,40},{40,48},{48,56},{56,64},{64,7... | collective-permute-start | bytes 98312 | tf_op jit(solution)/shard_map/while/body/eval_jaxpr/ppermute | solution.py:13
  785.4 13.9 %collective-permute-start = (bf16[2,1,4,2048]{3,2,1,0:T(4,128)(2,1)S(1)}, bf16[2,1,4,2048]{3,2,1,0:T(4,128)(2,1)S(1)}, u32[]{:S(2)}, u32[]{:S(2)}) collective-permute-start(bf16[2,1,4,2048]{3,2,1,0:T(4,128)(2,1)S(1)} %get-tuple-element.215), channel_id=1, source_target_pairs={{0,8},{8,16},{16,24},{24,32},{32,40},{40,48},{48,56},{56,64},{64,7... | collective-permute-start | bytes 98312 | tf_op jit(solution)/shard_map/while/body/eval_jaxpr/ppermute | solution.py:13
  800.2 13.9 %collective-permute-start = (bf16[2,1,4,2048]{3,2,1,0:T(4,128)(2,1)S(1)}, bf16[2,1,4,2048]{3,2,1,0:T(4,128)(2,1)S(1)}, u32[]{:S(2)}, u32[]{:S(2)}) collective-permute-start(bf16[2,1,4,2048]{3,2,1,0:T(4,128)(2,1)S(1)} %get-tuple-element.215), channel_id=1, source_target_pairs={{0,8},{8,16},{16,24},{24,32},{32,40},{40,48},{48,56},{56,64},{64,7... | collective-permute-start | bytes 98312 | tf_op jit(solution)/shard_map/while/body/eval_jaxpr/ppermute | solution.py:13
  815.0 14.1 %collective-permute-start = (bf16[2,1,4,2048]{3,2,1,0:T(4,128)(2,1)S(1)}, bf16[2,1,4,2048]{3,2,1,0:T(4,128)(2,1)S(1)}, u32[]{:S(2)}, u32[]{:S(2)}) collective-permute-start(bf16[2,1,4,2048]{3,2,1,0:T(4,128)(2,1)S(1)} %get-tuple-element.215), channel_id=1, source_target_pairs={{0,8},{8,16},{16,24},{24,32},{32,40},{40,48},{48,56},{56,64},{64,7... | collective-permute-start | bytes 98312 | tf_op jit(solution)/shard_map/while/body/eval_jaxpr/ppermute | solution.py:13
  829.9 18.4 %collective-permute-start = (bf16[2,1,4,2048]{3,2,1,0:T(4,128)(2,1)S(1)}, bf16[2,1,4,2048]{3,2,1,0:T(4,128)(2,1)S(1)}, u32[]{:S(2)}, u32[]{:S(2)}) collective-permute-start(bf16[2,1,4,2048]{3,2,1,0:T(4,128)(2,1)S(1)} %get-tuple-element.215), channel_id=1, source_target_pairs={{0,8},{8,16},{16,24},{24,32},{32,40},{40,48},{48,56},{56,64},{64,7... | collective-permute-start | bytes 98312 | tf_op jit(solution)/shard_map/while/body/eval_jaxpr/ppermute | solution.py:13
  849.1 14.1 %collective-permute-start = (bf16[2,1,4,2048]{3,2,1,0:T(4,128)(2,1)S(1)}, bf16[2,1,4,2048]{3,2,1,0:T(4,128)(2,1)S(1)}, u32[]{:S(2)}, u32[]{:S(2)}) collective-permute-start(bf16[2,1,4,2048]{3,2,1,0:T(4,128)(2,1)S(1)} %get-tuple-element.215), channel_id=1, source_target_pairs={{0,8},{8,16},{16,24},{24,32},{32,40},{40,48},{48,56},{56,64},{64,7... | collective-permute-start | bytes 98312 | tf_op jit(solution)/shard_map/while/body/eval_jaxpr/ppermute | solution.py:13
  864.0 14.7 %collective-permute-start = (bf16[2,1,4,2048]{3,2,1,0:T(4,128)(2,1)S(1)}, bf16[2,1,4,2048]{3,2,1,0:T(4,128)(2,1)S(1)}, u32[]{:S(2)}, u32[]{:S(2)}) collective-permute-start(bf16[2,1,4,2048]{3,2,1,0:T(4,128)(2,1)S(1)} %get-tuple-element.215), channel_id=1, source_target_pairs={{0,8},{8,16},{16,24},{24,32},{32,40},{40,48},{48,56},{56,64},{64,7... | collective-permute-start | bytes 98312 | tf_op jit(solution)/shard_map/while/body/eval_jaxpr/ppermute | solution.py:13
  879.6 14.6 %collective-permute-start = (bf16[2,1,4,2048]{3,2,1,0:T(4,128)(2,1)S(1)}, bf16[2,1,4,2048]{3,2,1,0:T(4,128)(2,1)S(1)}, u32[]{:S(2)}, u32[]{:S(2)}) collective-permute-start(bf16[2,1,4,2048]{3,2,1,0:T(4,128)(2,1)S(1)} %get-tuple-element.215), channel_id=1, source_target_pairs={{0,8},{8,16},{16,24},{24,32},{32,40},{40,48},{48,56},{56,64},{64,7... | collective-permute-start | bytes 98312 | tf_op jit(solution)/shard_map/while/body/eval_jaxpr/ppermute | solution.py:13
  909.8 14.1 %collective-permute-start = (bf16[2,1,4,2048]{3,2,1,0:T(4,128)(2,1)S(1)}, bf16[2,1,4,2048]{3,2,1,0:T(4,128)(2,1)S(1)}, u32[]{:S(2)}, u32[]{:S(2)}) collective-permute-start(bf16[2,1,4,2048]{3,2,1,0:T(4,128)(2,1)S(1)} %get-tuple-element.215), channel_id=1, source_target_pairs={{0,8},{8,16},{16,24},{24,32},{32,40},{40,48},{48,56},{56,64},{64,7... | collective-permute-start | bytes 98312 | tf_op jit(solution)/shard_map/while/body/eval_jaxpr/ppermute | solution.py:13
  924.7 16.1 %collective-permute-start = (bf16[2,1,4,2048]{3,2,1,0:T(4,128)(2,1)S(1)}, bf16[2,1,4,2048]{3,2,1,0:T(4,128)(2,1)S(1)}, u32[]{:S(2)}, u32[]{:S(2)}) collective-permute-start(bf16[2,1,4,2048]{3,2,1,0:T(4,128)(2,1)S(1)} %get-tuple-element.215), channel_id=1, source_target_pairs={{0,8},{8,16},{16,24},{24,32},{32,40},{40,48},{48,56},{56,64},{64,7... | collective-permute-start | bytes 98312 | tf_op jit(solution)/shard_map/while/body/eval_jaxpr/ppermute | solution.py:13
  (16 other events, 217.5 us)
where the time goes:
time: 1130 us
  waiting for transfers between devices  770 us (68%)
  blocking collectives  146 us (13%)
  starting transfers between devices  121 us (11%)
  other arithmetic  61.1 us (5%)
  matrix products  12.9 us (1%)
    ppermute x63, waiting for transfers between devices, passed_along(): lax.ppermute(array, axis, [(i, (i + by) % devices) for i in range(devices)])  770 us
    unnamed x1, blocking collectives  146 us
    ppermute x63, starting transfers between devices, passed_along(): lax.ppermute(array, axis, [(i, (i + by) % devices) for i in range(devices)])  121 us
    dynamic_update_slice x64, other arithmetic, place(): return lax.dynamic_update_slice(stack_buffer, cross_spec, starts)  44.9 us
  transfers between devices with their start and end apart: 63, of which 63 were waited for; matrix products, arithmetic and copies ran while one was open for 0% of the time, Pallas kernels for 0%

commit v1 on v0

v1 whole, which is shorter than its diff:
```python
import functools
import math

import jax
import jax.numpy as jnp
import ml_dtypes
import numpy as np
from jax import lax
from jax.experimental import pallas as pl
from jax.experimental.pallas import tpu as pltpu
from jax.sharding import Mesh, PartitionSpec as P

LAGS = 256
BINS = 2048
CHUNK = 256
GRID = (("zl", 8), ("x", 4), ("core", 2), ("y", 4), ("zh", 2))
STA = ("zl", "x", "core")
WIN = ("y", "zh")


def lag_table():
    phase = np.arange(BINS)[:, None] * (np.arange(LAGS)[None, :] - LAGS // 2) % (2 * BINS)
    angles = phase.astype(np.float32) * np.float32(math.pi / BINS)
    scale = np.float32(1.0 / math.sqrt(BINS))
    both = np.concatenate([np.cos(angles), -np.sin(angles)], axis=0).astype(np.float32) * scale
    return both.astype(ml_dtypes.bfloat16)


def whiten(spectra, quality):
    values = spectra.astype(jnp.float32)
    power_mean = jnp.mean(values[0] * values[0] + values[1] * values[1], axis=-1, keepdims=True)
    flags = quality.astype(jnp.float32)[:, :, None]
    return (values * (lax.rsqrt(power_mean + 1e-06) * flags)[None]).astype(jnp.bfloat16)


def pair_kernel(half_ref, far_ref, own_ref, table_ref, out_ref, far_re, far_im, own, cross, total, order):
    second = half_ref[0] == 1
    for w in range(2):
        for k in range(4):
            both = far_ref[pl.ds((w * 8 + 2 * k) * 8, 16), :].astype(jnp.float32)
            block = jnp.where(second, both[8:16], both[0:8])
            far_re[w, 4 * k : 4 * k + 4, :] = block[0:4]
            far_im[w, 4 * k : 4 * k + 4, :] = block[4:8]
    own[...] = own_ref[...].astype(jnp.float32)
    total[...] = jnp.zeros_like(total)

    @pl.loop(0, BINS // CHUNK)
    def _(c):
        at = pl.multiple_of(c * CHUNK, CHUNK)
        bins = pl.ds(at, CHUNK)

        @pl.loop(0, 8)
        def _(block):
            first = pl.multiple_of(block * 16, 16)
            b_re = [far_re[w, :, bins] for w in range(2)]
            b_im = [far_im[w, :, bins] for w in range(2)]
            for i in range(4):
                re, im = None, None
                for w in range(2):
                    a_re = own[pl.ds(first + w * 8 + i, 1), bins]
                    a_im = own[pl.ds(first + w * 8 + 4 + i, 1), bins]
                    re_w = a_re * b_re[w] + a_im * b_im[w]
                    im_w = a_im * b_re[w] - a_re * b_im[w]
                    re = re_w if re is None else re + re_w
                    im = im_w if im is None else im + im_w
                rows = pl.ds(pl.multiple_of(block * 64 + i * 16, 16), 16)
                cross[rows, 0:CHUNK] = re.astype(jnp.bfloat16)
                cross[rows, CHUNK : 2 * CHUNK] = im.astype(jnp.bfloat16)

        total[...] += jnp.dot(
            cross[:, 0:CHUNK], table_ref[bins, :], preferred_element_type=jnp.float32
        ) + jnp.dot(
            cross[:, CHUNK : 2 * CHUNK],
            table_ref[pl.ds(pl.multiple_of(BINS + at, CHUNK), CHUNK), :],
            preferred_element_type=jnp.float32,
        )

    for block in range(8):
        for i in range(4):
            rows = total[block * 64 + i * 16 : block * 64 + i * 16 + 16, :]
            for k in range(4):
                to = (block * 4 + k) * 16 + i * 4
                order[to : to + 4, :] = rows[4 * k : 4 * k + 4]
    out_ref[...] = order[...].astype(jnp.bfloat16)


def pairs(half, far, own, table):
    vmem = pl.BlockSpec(memory_space=pltpu.VMEM)
    return pl.pallas_call(
        pair_kernel,
        out_shape=jax.ShapeDtypeStruct((512, LAGS), jnp.bfloat16),
        in_specs=[pl.BlockSpec(memory_space=pltpu.SMEM), vmem, vmem, vmem],
        out_specs=vmem,
        scratch_shapes=[
            pltpu.VMEM((2, 16, BINS), jnp.float32),
            pltpu.VMEM((2, 16, BINS), jnp.float32),
            pltpu.VMEM((128, BINS), jnp.float32),
            pltpu.VMEM((512, 2 * CHUNK), jnp.bfloat16),
            pltpu.VMEM((512, LAGS), jnp.float32),
            pltpu.VMEM((512, LAGS), jnp.float32),
        ],
        compiler_params=pltpu.CompilerParams(vmem_limit_bytes=32 * 1024 * 1024),
    )(half, far, own, table)


def shards(table, spectra, quality, block_mask):
    white = whiten(spectra, quality).reshape(8, BINS)
    column = lax.all_gather(white, ("zh", "zl"))
    zl = lax.axis_index("zl")
    mine = lax.dynamic_slice_in_dim(column.reshape(2, 8, 8, BINS), zl, 1, axis=1)
    plane = lax.all_gather(mine.reshape(16, BINS), ("x", "core"))
    half = lax.axis_index("zh").astype(jnp.int32).reshape(1)
    partial = pairs(half, column.reshape(128, BINS), plane.reshape(128, BINS), table)
    parts = lax.all_to_all(partial.reshape(32, 16, LAGS), ("x", "core", "y"), 0, 0, tiled=True)
    summed = jnp.sum(parts.astype(jnp.float32).reshape(8, 4, 4, 4, LAGS), axis=1)
    group = lax.axis_index(WIN)
    mask = lax.dynamic_slice_in_dim(block_mask[0], group * 8, 8).astype(jnp.float32)
    summed = summed * mask[:, None, None, None]
    return summed.transpose(1, 0, 2, 3).reshape(4, 32, LAGS).astype(jnp.bfloat16)


def solution(mesh):
    names, sizes = zip(*GRID)
    fine = Mesh(mesh.devices.reshape(sizes), names)
    placed = (P(None, WIN, STA, None), P(WIN, STA), P(STA, None))
    table = lag_table()

    def run(spectra, quality, block_mask):
        body = functools.partial(shards, jnp.asarray(table))
        return jax.shard_map(
            body, mesh=fine, in_specs=placed, out_specs=P(STA, WIN, None), check_vma=False
        )(spectra, quality, block_mask)

    return run
```

time: 1130 us -> 80.3 us (0.07)
  the two profiles are of different devices: /device:TPU:24 before, /device:TPU:1 now
where the time goes in v1:
time: 80.3 us; the launch traced here: 80 us
  blocking collectives  53.3 us (66%)
  waiting for transfers between devices  8.71 us (11%)
  starting transfers between devices  6.63 us (8%)
  Pallas kernels  6.14 us (8%)
  other arithmetic  2.69 us (3%)
  local copies, waits for them, and re-layouts  2.42 us (3%)
    all_gather x1, blocking collectives, shards(): column = lax.all_gather(white, ('zh', 'zl'))  31.8 us
    all_gather x1, blocking collectives, shards(): plane = lax.all_gather(mine.reshape(16, BINS), ('x', 'core'))  21.5 us
    all_to_all x1, waiting for transfers between devices, shards(): lax.all_to_all(partial.reshape(32, 16, LAGS), ('x', 'core', 'y'), 0, 0, t...  8.71 us
    all_to_all x1, starting transfers between devices, shards(): lax.all_to_all(partial.reshape(32, 16, LAGS), ('x', 'core', 'y'), 0, 0, t...  6.63 us
    pallas_call x1, Pallas kernels, pairs(): pl.pallas_call(pair_kernel, out_shape=jax.ShapeDtypeStruct((512, LAGS), j...  6.14 us
    unnamed x4, local copies, waits for them, and re-layouts  1.61 us
  transfers between devices with their start and end apart: 1, of which 1 were waited for; matrix products, arithmetic and copies ran while one was open for 0% of the time, Pallas kernels for 0%

profile of v1, /device:TPU:1, one launch (start us, length us, event | category | flops | bytes accessed | tf_op | source)
XLA Modules:
  0.0 80.0 jit_solution(1585398516336829647)
XLA Ops:
  0.0 0.8 convert_element_type.29
  0.8 0.1 fusion.2
  0.9 0.7 bitcast_multiply_fusion
  1.6 0.8 %multiply_convert_fusion.1 = bf16[2,1,4,2048]{3,2,1,0:T(4,128)(2,1)S(1)} fusion(f32[4]{0:T(128)S(1)} %bitcast_multiply_fusion, bf16[2,1,4,2048]{3,2,1,0:T(4,128)(2,1)} %param.4), kind=kLoop, calls=%fused_computation.3 | loop fusion | flops 49152 | bytes 65552 | tf_op jit(solution)/shard_map/convert_element_type | solution.py:33
  2.4 31.8 %all_gather.6 = bf16[16,8,2048]{2,1,0:T(8,128)(2,1)S(1)} all-gather(bf16[1,8,2048]{2,1,0:T(8,128)(2,1)S(1)} %all_gather_reshape.6), channel_id=1, replica_groups=mesh['zl'=8,'x'=4,'core'=2,'y'=4,'zh'=2] {'zh','zl'}, dimensions={0}, use_global_device_ids=true | all-gather | bytes 557056 | tf_op jit(solution)/shard_map/all_gather | solution.py:108
  34.2 21.5 %all_gather.7 = bf16[8,16,2048]{2,1,0:T(8,128)(2,1)S(1)} all-gather(bf16[1,16,2048]{2,1,0:T(8,128)(2,1)S(1)} %dynamic-slice_bitcast_fusion), channel_id=1, replica_groups=mesh['zl'=8,'x'=4,'core'=2,'y'=4,'zh'=2] {'x','core'}, dimensions={0}, use_global_device_ids=true | all-gather | bytes 589824 | tf_op jit(solution)/shard_map/all_gather | solution.py:111
  55.7 0.0 copy-start.1
  55.7 0.0 copy-start
  55.7 1.6 %copy-done = bf16[4096,256]{1,0:T(8,128)(2,1)S(1)} copy-done((bf16[4096,256]{1,0:T(8,128)(2,1)S(1)}, bf16[4096,256]{1,0:T(8,128)(2,1)}, u32[]{:S(2)}) %copy-start) | copy-done | bytes 2097176
  57.4 6.1 %shard_map.46 = bf16[512,256]{1,0:T(8,128)(2,1)} custom-call(s32[1]{0:T(128)} %bitcast.half_ref, bf16[128,2048]{1,0:T(8,128)(2,1)S(1)} %bitcast.15, bf16[128,2048]{1,0:T(8,128)(2,1)S(1)} %bitcast.16, bf16[4096,256]{1,0:T(8,128)(2,1)S(1)} %copy-done), custom_call_target="tpu_custom_call" | custom-call | tf_op jit(solution)/shard_map/pallas_call | solution.py:89
  63.5 6.6 %all-to-all-start = ((bf16[32,16,256]{2,1,0:T(8,128)(2,1)}), bf16[32,16,256]{2,1,0:T(8,128)(2,1)S(1)}, u32[]{:S(2)}, u32[]{:S(2)}) async-start(bf16[32,16,256]{2,1,0:T(8,128)(2,1)} %bitcast.6), calls=%async_computation | async-start | bytes 524288 | tf_op jit(solution)/shard_map/all_to_all | solution.py:114
  70.1 0.0 copy-done.1
  70.1 0.1 convert_bitcast_fusion
  70.2 8.7 %all-to-all-done = bf16[32,16,256]{2,1,0:T(8,128)(2,1)S(1)} async-done(((bf16[32,16,256]{2,1,0:T(8,128)(2,1)}), bf16[32,16,256]{2,1,0:T(8,128)(2,1)S(1)}, u32[]{:S(2)}, u32[]{:S(2)}) %all-to-all-start) | async-done | bytes 262176 | tf_op jit(solution)/shard_map/all_to_all | solution.py:114
  78.9 0.1 reshape.91
  79.1 0.1 reduce_sum.19
  79.2 0.1 fusion
  79.3 0.6 copy.7
  (3 shorter events, 0.0 us)
Async XLA Ops:
  55.7 14.4 %copy-start.1 = (s32[1,64]{1,0:T(1,128)S(1)}, s32[1,64]{1,0:T(1,128)}, u32[]{:S(2)}) copy-start(s32[1,64]{1,0:T(1,128)} %param.6) | copy-start | bytes 772
  55.7 1.6 %copy-start = (bf16[4096,256]{1,0:T(8,128)(2,1)S(1)}, bf16[4096,256]{1,0:T(8,128)(2,1)}, u32[]{:S(2)}) copy-start(bf16[4096,256]{1,0:T(8,128)(2,1)} %constant.32.clone.table_ref) | copy-start | bytes 6291460
  63.5 15.4 %all-to-all-start = ((bf16[32,16,256]{2,1,0:T(8,128)(2,1)}), bf16[32,16,256]{2,1,0:T(8,128)(2,1)S(1)}, u32[]{:S(2)}, u32[]{:S(2)}) async-start(bf16[32,16,256]{2,1,0:T(8,128)(2,1)} %bitcast.6), calls=%async_computation | async-start | bytes 524288 | tf_op jit(solution)/shard_map/all_to_all | solution.py:114

commit v2 on v1

v2 whole, which is shorter than its diff:
```python
import functools
import math

import jax
import jax.numpy as jnp
import ml_dtypes
import numpy as np
from jax import lax
from jax.experimental import pallas as pl
from jax.experimental.pallas import tpu as pltpu
from jax.sharding import Mesh, PartitionSpec as P

LAGS = 256
BINS = 2048
CHUNK = 256
CHUNKS = BINS // CHUNK
GRID = (("zl", 8), ("x", 4), ("core", 2), ("y", 4), ("zh", 2))
STA = ("zl", "x", "core")
WIN = ("y", "zh")
VMEM = pl.BlockSpec(memory_space=pltpu.VMEM)
SMEM = pl.BlockSpec(memory_space=pltpu.SMEM)


def lag_table():
    phase = np.arange(BINS)[:, None] * (np.arange(LAGS)[None, :] - LAGS // 2) % (2 * BINS)
    angles = phase.astype(np.float32) * np.float32(math.pi / BINS)
    scale = np.float32(1.0 / math.sqrt(BINS))
    both = np.stack([np.cos(angles), -np.sin(angles)]).astype(np.float32) * scale
    both = both.reshape(2, CHUNKS, CHUNK, LAGS).transpose(1, 0, 2, 3).reshape(2 * BINS, LAGS)
    return both.astype(ml_dtypes.bfloat16)


def whiten_kernel(quality_ref, spectra_ref, white_ref):
    re = spectra_ref[0, 0].astype(jnp.float32)
    im = spectra_ref[1, 0].astype(jnp.float32)
    power_mean = jnp.mean(re * re + im * im, axis=-1, keepdims=True)
    row = lax.broadcasted_iota(jnp.int32, (4, 1), 0)
    flags = jnp.zeros((4, 1), jnp.float32)
    for s in range(4):
        flags = jnp.where(row == s, quality_ref[0, s].astype(jnp.float32), flags)
    scale = lax.rsqrt(power_mean + 1e-06) * flags
    white_ref[...] = jnp.concatenate([re * scale, im * scale], axis=0).astype(jnp.bfloat16)


def whiten(spectra, quality):
    return pl.pallas_call(
        whiten_kernel,
        out_shape=jax.ShapeDtypeStruct((8, BINS), jnp.bfloat16),
        in_specs=[SMEM, VMEM],
        out_specs=VMEM,
    )(quality, spectra)


def pair_kernel(
    place_ref, mine_ref, other_ref, own_ref, table_hbm, out_ref,
    far_re, far_im, own, cross_even, cross_odd, total, order, table, arrived,
):
    fetch = pltpu.make_async_copy(table_hbm, table, arrived)
    fetch.start()
    second = place_ref[0] == 1
    core = place_ref[1]
    for column_ref, side in ((mine_ref, core), (other_ref, 1 - core)):
        for w in range(2):
            for k in range(4):
                both = column_ref[pl.ds((w * 8 + 2 * k) * 8, 16), :].astype(jnp.float32)
                block = jnp.where(second, both[8:16], both[0:8])
                far_re[side, w, 4 * k : 4 * k + 4, :] = block[0:4]
                far_im[side, w, 4 * k : 4 * k + 4, :] = block[4:8]
    own[...] = own_ref[...].astype(jnp.float32)
    total[...] = jnp.zeros_like(total)

    def products(c, cross):
        bins = pl.ds(pl.multiple_of(c * CHUNK, CHUNK), CHUNK)
        for side in range(2):
            b_re = [far_re[side, w, :, bins] for w in range(2)]
            b_im = [far_im[side, w, :, bins] for w in range(2)]
            for i in range(16):
                re, im = None, None
                for w in range(2):
                    at = (i // 4) * 16 + w * 8 + i % 4
                    a_re = own[at : at + 1, bins]
                    a_im = own[at + 4 : at + 5, bins]
                    re_w = a_re * b_re[w] + a_im * b_im[w]
                    im_w = a_im * b_re[w] - a_re * b_im[w]
                    re = re_w if re is None else re + re_w
                    im = im_w if im is None else im + im_w
                to = side * 256 + i * 16
                cross[to : to + 16, 0:CHUNK] = re.astype(jnp.bfloat16)
                cross[to : to + 16, CHUNK : 2 * CHUNK] = im.astype(jnp.bfloat16)

    def to_lags(c, cross):
        rows = pl.ds(pl.multiple_of(c * 2 * CHUNK, 2 * CHUNK), 2 * CHUNK)
        total[...] += jnp.dot(cross[...], table[rows, :], preferred_element_type=jnp.float32)

    products(0, cross_even)
    fetch.wait()

    @pl.loop(0, CHUNKS // 2 - 1)
    def _(c):
        products(2 * c + 1, cross_odd)
        to_lags(2 * c, cross_even)
        products(2 * c + 2, cross_even)
        to_lags(2 * c + 1, cross_odd)

    products(CHUNKS - 1, cross_odd)
    to_lags(CHUNKS - 2, cross_even)
    to_lags(CHUNKS - 1, cross_odd)

    for side in range(2):
        for i in range(16):
            rows = total[side * 256 + i * 16 : side * 256 + i * 16 + 16, :]
            for k in range(4):
                to = ((i // 4) * 4 + k) * 32 + (i % 4) * 8 + side * 4
                order[to : to + 4, :] = rows[4 * k : 4 * k + 4]
    out_ref[...] = order[...].astype(jnp.bfloat16)


def pairs(place, mine, other, own, table):
    return pl.pallas_call(
        pair_kernel,
        out_shape=jax.ShapeDtypeStruct((512, LAGS), jnp.bfloat16),
        in_specs=[SMEM, VMEM, VMEM, VMEM, pl.BlockSpec(memory_space=pl.ANY)],
        out_specs=VMEM,
        scratch_shapes=[
            pltpu.VMEM((2, 2, 16, BINS), jnp.float32),
            pltpu.VMEM((2, 2, 16, BINS), jnp.float32),
            pltpu.VMEM((64, BINS), jnp.float32),
            pltpu.VMEM((512, 2 * CHUNK), jnp.bfloat16),
            pltpu.VMEM((512, 2 * CHUNK), jnp.bfloat16),
            pltpu.VMEM((512, LAGS), jnp.float32),
            pltpu.VMEM((512, LAGS), jnp.float32),
            pltpu.VMEM((2 * BINS, LAGS), jnp.bfloat16),
            pltpu.SemaphoreType.DMA,
        ],
        compiler_params=pltpu.CompilerParams(vmem_limit_bytes=40 * 1024 * 1024),
    )(place, mine, other, own, table)


def finish_kernel(group_ref, mask_ref, parts_ref, out_ref):
    first = group_ref[0] * 8
    upper = lax.broadcasted_iota(jnp.int32, (8, 1), 0) < 4
    for pair in range(2):
        sums, masks = [], []
        for x in (2 * pair, 2 * pair + 1):
            total = None
            for y in range(4):
                part = parts_ref[(x * 4 + y) * 32 : (x * 4 + y) * 32 + 32, :].astype(jnp.float32)
                total = part if total is None else total + part
            sums.append(total)
            masks.append(
                jnp.where(
                    upper,
                    mask_ref[0, first + 2 * x].astype(jnp.float32),
                    mask_ref[0, first + 2 * x + 1].astype(jnp.float32),
                )
            )
        for i in range(4):
            rows = jnp.concatenate([s[8 * i : 8 * i + 8] * m for s, m in zip(sums, masks)], axis=0)
            out_ref[i, 16 * pair : 16 * pair + 16, :] = rows.astype(jnp.bfloat16)


def finish(group, block_mask, parts):
    return pl.pallas_call(
        finish_kernel,
        out_shape=jax.ShapeDtypeStruct((4, 32, LAGS), jnp.bfloat16),
        in_specs=[SMEM, SMEM, VMEM],
        out_specs=VMEM,
    )(group, block_mask, parts)


def shards(table, spectra, quality, block_mask):
    white = whiten(spectra, quality)
    column = lax.all_gather(white, ("zh", "zl"))
    other = lax.ppermute(column, "core", [(0, 1), (1, 0)])
    zl = lax.axis_index("zl")
    own = lax.dynamic_slice_in_dim(column.reshape(2, 8, 8, BINS), zl, 1, axis=1)
    plane = lax.all_gather(own.reshape(16, BINS), "x")
    place = jnp.stack([lax.axis_index("zh"), lax.axis_index("core")]).astype(jnp.int32)
    partial = pairs(
        place, column.reshape(128, BINS), other.reshape(128, BINS), plane.reshape(64, BINS), table
    )
    parts = lax.all_to_all(partial.reshape(16, 32, LAGS), ("x", "y"), 0, 0, tiled=True)
    group = lax.axis_index(WIN).astype(jnp.int32).reshape(1)
    return finish(group, block_mask, parts.reshape(512, LAGS))


def solution(mesh):
    names, sizes = zip(*GRID)
    fine = Mesh(mesh.devices.reshape(sizes), names)
    placed = (P(None, WIN, STA, None), P(WIN, STA), P(STA, None))
    table = lag_table()

    def run(spectra, quality, block_mask):
        body = functools.partial(shards, jnp.asarray(table))
        return jax.shard_map(
            body, mesh=fine, in_specs=placed, out_specs=P(STA, WIN, None), check_vma=False
        )(spectra, quality, block_mask)

    return run
```

time: 80.3 us -> 77.5 us (0.965)
  the two profiles are of different devices: /device:TPU:1 before, /device:TPU:8 now
where the time goes in v2:
time: 77.5 us; the launch traced here: 77.2 us
  blocking collectives  51.4 us (66%)
  starting transfers between devices  8.79 us (11%)
  Pallas kernels  7.59 us (10%)
  waiting for transfers between devices  6.98 us (9%)
  local copies, waits for them, and re-layouts  2.29 us (3%)
    all_gather x1, blocking collectives, shards(): column = lax.all_gather(white, ('zh', 'zl'))  38.8 us
    all_gather x1, blocking collectives, shards(): plane = lax.all_gather(own.reshape(16, BINS), 'x')  12.6 us
    all_to_all x1, waiting for transfers between devices, shards(): lax.all_to_all(partial.reshape(16, 32, LAGS), ('x', 'y'), 0, 0, tiled=True)  6.98 us
    all_to_all x1, starting transfers between devices, shards(): lax.all_to_all(partial.reshape(16, 32, LAGS), ('x', 'y'), 0, 0, tiled=True)  6.88 us
    pallas_call x1, Pallas kernels, pairs(): pl.pallas_call(pair_kernel, out_shape=jax.ShapeDtypeStruct((512, LAGS), j...  4.46 us
    unnamed x4, local copies, waits for them, and re-layouts  2.28 us
    ppermute x1, starting transfers between devices, shards(): other = lax.ppermute(column, 'core', [(0, 1), (1, 0)])  1.91 us
    pallas_call x1, Pallas kernels, finish(): pl.pallas_call(finish_kernel, out_shape=jax.ShapeDtypeStruct((4, 32, LAGS...  1.63 us
  transfers between devices with their start and end apart: 2, of which 1 were waited for; matrix products, arithmetic and copies ran while one was open for 0% of the time, Pallas kernels for 0%

profile of v2, /device:TPU:8, one launch (start us, length us, event | category | flops | bytes accessed | tf_op | source)
XLA Modules:
  0.0 77.2 jit_solution(12982951825791175582)
XLA Ops:
  0.0 1.5 %shard_map.46 = bf16[8,2048]{1,0:T(8,128)(2,1)} custom-call(s32[1,4]{1,0:T(1,128)} %quality_ref.1, bf16[2,1,4,2048]{3,2,1,0:T(4,128)(2,1)} %spectra_ref.1), custom_call_target="tpu_custom_call" | custom-call | tf_op jit(solution)/shard_map/pallas_call | solution.py:46
  1.5 38.8 %all-gather.mine_ref = bf16[128,2048]{1,0:T(8,128)(2,1)S(1)} all-gather(bf16[8,2048]{1,0:T(8,128)(2,1)} %shard_map.46), channel_id=2, replica_groups=mesh['zl'=8,'x'=4,'core'=2,'y'=4,'zh'=2] {'zh','zl'}, dimensions={0}, use_global_device_ids=true | all-gather | bytes 557056 | tf_op jit(solution)/shard_map/all_gather | solution.py:173
  40.3 1.9 %collective-permute-start = (bf16[16,8,2048]{2,1,0:T(8,128)(2,1)S(1)}, bf16[16,8,2048]{2,1,0:T(8,128)(2,1)S(1)}, u32[]{:S(2)}, u32[]{:S(2)}) collective-permute-start(bf16[16,8,2048]{2,1,0:T(8,128)(2,1)S(1)} %bitcast.11), channel_id=1, source_target_pairs={{0,8},{8,0},{1,9},{9,1},{2,10},{10,2},{3,11},{11,3},{4,12},{12,4},... | collective-permute-start | bytes 1572872 | tf_op jit(solution)/shard_map/ppermute | solution.py:174
  42.2 12.6 %all_gather.11 = bf16[4,16,2048]{2,1,0:T(8,128)(2,1)S(1)} all-gather(bf16[1,16,2048]{2,1,0:T(8,128)(2,1)S(1)} %dynamic-slice_bitcast_fusion), channel_id=1, replica_groups=mesh['zl'=8,'x'=4,'core'=2,'y'=4,'zh'=2] {'x'}, dimensions={0}, use_global_device_ids=true | all-gather | bytes 327680 | tf_op jit(solution)/shard_map/all_gather | solution.py:177
  54.8 0.1 pad_add_fusion.place_ref
  54.9 0.0 collective-permute-done
  54.9 0.0 copy-start
  54.9 1.6 %copy-done = bf16[4096,256]{1,0:T(8,128)(2,1)S(1)} copy-done((bf16[4096,256]{1,0:T(8,128)(2,1)S(1)}, bf16[4096,256]{1,0:T(8,128)(2,1)}, u32[]{:S(2)}) %copy-start) | copy-done | bytes 2097176
  56.5 4.5 %shard_map.47 = bf16[512,256]{1,0:T(8,128)(2,1)} custom-call(s32[2]{0:T(128)S(1)} %pad_add_fusion.place_ref, bf16[128,2048]{1,0:T(8,128)(2,1)S(1)} %all-gather.mine_ref, bf16[128,2048]{1,0:T(8,128)(2,1)S(1)} %bitcast.14, bf16[64,2048]{1,0:T(8,128)(2,1)S(1)} %bitcast.13, bf16[4096,256]{1,0:T(8,128)(2,1)S(1)} %copy-done), custom_call_target="tpu_custom_call" | custom-call | tf_op jit(solution)/shard_map/pallas_call | solution.py:119
  61.0 6.9 %all-to-all-start = ((bf16[16,32,256]{2,1,0:T(8,128)(2,1)}), bf16[16,32,256]{2,1,0:T(8,128)(2,1)S(1)}, u32[]{:S(2)}, u32[]{:S(2)}) async-start(bf16[16,32,256]{2,1,0:T(8,128)(2,1)} %bitcast.8), calls=%async_computation | async-start | bytes 524288 | tf_op jit(solution)/shard_map/all_to_all | solution.py:182
  67.9 7.0 %all-to-all-done = bf16[16,32,256]{2,1,0:T(8,128)(2,1)S(1)} async-done(((bf16[16,32,256]{2,1,0:T(8,128)(2,1)}), bf16[16,32,256]{2,1,0:T(8,128)(2,1)S(1)}, u32[]{:S(2)}, u32[]{:S(2)}) %all-to-all-start) | async-done | bytes 262176 | tf_op jit(solution)/shard_map/all_to_all | solution.py:182
  74.8 0.0 copy-start.1
  74.8 0.7 copy-done.1
  75.5 1.6 %shard_map.48 = bf16[4,32,256]{2,1,0:T(8,128)(2,1)} custom-call(s32[1]{0:T(128)} %bitcast.group_ref, s32[1,64]{1,0:T(1,128)} %mask_ref.1, bf16[512,256]{1,0:T(8,128)(2,1)} %bitcast.15), custom_call_target="tpu_custom_call" | custom-call | tf_op jit(solution)/shard_map/pallas_call | solution.py:163
  (1 shorter events, 0.0 us)
Async XLA Ops:
  40.3 14.6 %collective-permute-start = (bf16[16,8,2048]{2,1,0:T(8,128)(2,1)S(1)}, bf16[16,8,2048]{2,1,0:T(8,128)(2,1)S(1)}, u32[]{:S(2)}, u32[]{:S(2)}) collective-permute-start(bf16[16,8,2048]{2,1,0:T(8,128)(2,1)S(1)} %bitcast.11), channel_id=1, source_target_pairs={{0,8},{8,0},{1,9},{9,1},{2,10},{10,2},{3,11},{11,3},{4,12},{12,4},... | collective-permute-start | bytes 1572872 | tf_op jit(solution)/shard_map/ppermute | solution.py:174
  54.9 1.6 %copy-start = (bf16[4096,256]{1,0:T(8,128)(2,1)S(1)}, bf16[4096,256]{1,0:T(8,128)(2,1)}, u32[]{:S(2)}) copy-start(bf16[4096,256]{1,0:T(8,128)(2,1)} %constant.24.clone.table_hbm) | copy-start | bytes 6291460
  61.0 13.9 %all-to-all-start = ((bf16[16,32,256]{2,1,0:T(8,128)(2,1)}), bf16[16,32,256]{2,1,0:T(8,128)(2,1)S(1)}, u32[]{:S(2)}, u32[]{:S(2)}) async-start(bf16[16,32,256]{2,1,0:T(8,128)(2,1)} %bitcast.8), calls=%async_computation | async-start | bytes 524288 | tf_op jit(solution)/shard_map/all_to_all | solution.py:182
  74.8 0.7 copy-start.1

commit v3 on v2

--- a/solution.py
+++ b/solution.py
@@ -19,6 +19,7 @@
 WIN = ("y", "zh")
 VMEM = pl.BlockSpec(memory_space=pltpu.VMEM)
 SMEM = pl.BlockSpec(memory_space=pltpu.SMEM)
+SMALL = pltpu.CompilerParams(vmem_limit_bytes=4 * 1024 * 1024)
 
 
 def lag_table():
@@ -51,29 +52,45 @@
     )(quality, spectra)
 
 
+def choose_kernel(half_ref, column_ref, sent_ref, chosen_ref):
+    second = half_ref[0] == 1
+    for w in range(2):
+        parts = []
+        for k in range(4):
+            both = column_ref[(w * 8 + 2 * k) * 8 : (w * 8 + 2 * k) * 8 + 16, :].astype(jnp.float32)
+            parts.append(jnp.where(second, both[8:16], both[0:8]))
+        for c in range(2):
+            rows = jnp.concatenate([p[4 * c : 4 * c + 4] for p in parts], axis=0)
+            chosen_ref[(w * 2 + c) * 16 : (w * 2 + c) * 16 + 16, :] = rows.astype(jnp.bfloat16)
+
+
+def choose(half, column, sent):
+    return pl.pallas_call(
+        choose_kernel,
+        out_shape=jax.ShapeDtypeStruct((64, BINS), jnp.bfloat16),
+        in_specs=[SMEM, VMEM, pl.BlockSpec(memory_space=pl.ANY)],
+        out_specs=VMEM,
+        compiler_params=SMALL,
+    )(half, column, sent)
+
+
 def pair_kernel(
-    place_ref, mine_ref, other_ref, own_ref, table_hbm, out_ref,
-    far_re, far_im, own, cross_even, cross_odd, total, order, table, arrived,
+    core_ref, mine_ref, other_ref, own_ref, table_hbm, out_ref,
+    far, own, cross_even, cross_odd, total, order, table, arrived,
 ):
     fetch = pltpu.make_async_copy(table_hbm, table, arrived)
     fetch.start()
-    second = place_ref[0] == 1
-    core = place_ref[1]
-    for column_ref, side in ((mine_ref, core), (other_ref, 1 - core)):
-        for w in range(2):
-            for k in range(4):
-                both = column_ref[pl.ds((w * 8 + 2 * k) * 8, 16), :].astype(jnp.float32)
-                block = jnp.where(second, both[8:16], both[0:8])
-                far_re[side, w, 4 * k : 4 * k + 4, :] = block[0:4]
-                far_im[side, w, 4 * k : 4 * k + 4, :] = block[4:8]
+    core = core_ref[0]
+    far[core] = mine_ref[...].astype(jnp.float32)
+    far[1 - core] = other_ref[...].astype(jnp.float32)
     own[...] = own_ref[...].astype(jnp.float32)
     total[...] = jnp.zeros_like(total)
 
     def products(c, cross):
         bins = pl.ds(pl.multiple_of(c * CHUNK, CHUNK), CHUNK)
         for side in range(2):
-            b_re = [far_re[side, w, :, bins] for w in range(2)]
-            b_im = [far_im[side, w, :, bins] for w in range(2)]
+            b_re = [far[side, 32 * w : 32 * w + 16, bins] for w in range(2)]
+            b_im = [far[side, 32 * w + 16 : 32 * w + 32, bins] for w in range(2)]
             for i in range(16):
                 re, im = None, None
                 for w in range(2):
@@ -115,15 +132,14 @@
     out_ref[...] = order[...].astype(jnp.bfloat16)
 
 
-def pairs(place, mine, other, own, table):
+def pairs(core, mine, other, own, table):
     return pl.pallas_call(
         pair_kernel,
         out_shape=jax.ShapeDtypeStruct((512, LAGS), jnp.bfloat16),
         in_specs=[SMEM, VMEM, VMEM, VMEM, pl.BlockSpec(memory_space=pl.ANY)],
         out_specs=VMEM,
         scratch_shapes=[
-            pltpu.VMEM((2, 2, 16, BINS), jnp.float32),
-            pltpu.VMEM((2, 2, 16, BINS), jnp.float32),
+            pltpu.VMEM((2, 64, BINS), jnp.float32),
             pltpu.VMEM((64, BINS), jnp.float32),
             pltpu.VMEM((512, 2 * CHUNK), jnp.bfloat16),
             pltpu.VMEM((512, 2 * CHUNK), jnp.bfloat16),
@@ -133,7 +149,7 @@
             pltpu.SemaphoreType.DMA,
         ],
         compiler_params=pltpu.CompilerParams(vmem_limit_bytes=40 * 1024 * 1024),
-    )(place, mine, other, own, table)
+    )(core, mine, other, own, table)
 
 
 def finish_kernel(group_ref, mask_ref, parts_ref, out_ref):
@@ -165,20 +181,22 @@
         out_shape=jax.ShapeDtypeStruct((4, 32, LAGS), jnp.bfloat16),
         in_specs=[SMEM, SMEM, VMEM],
         out_specs=VMEM,
+        compiler_params=SMALL,
     )(group, block_mask, parts)
 
 
 def shards(table, spectra, quality, block_mask):
     white = whiten(spectra, quality)
     column = lax.all_gather(white, ("zh", "zl"))
-    other = lax.ppermute(column, "core", [(0, 1), (1, 0)])
     zl = lax.axis_index("zl")
     own = lax.dynamic_slice_in_dim(column.reshape(2, 8, 8, BINS), zl, 1, axis=1)
-    plane = lax.all_gather(own.reshape(16, BINS), "x")
-    place = jnp.stack([lax.axis_index("zh"), lax.axis_index("core")]).astype(jnp.int32)
-    partial = pairs(
-        place, column.reshape(128, BINS), other.reshape(128, BINS), plane.reshape(64, BINS), table
-    )
+    copies = jnp.broadcast_to(own.reshape(1, 16, BINS), (4, 16, BINS))
+    plane = lax.all_to_all(copies, "x", 0, 0, tiled=True)
+    half = lax.axis_index("zh").astype(jnp.int32).reshape(1)
+    core = lax.axis_index("core").astype(jnp.int32).reshape(1)
+    mine = choose(half, column.reshape(128, BINS), copies)
+    other = lax.ppermute(mine, "core", [(0, 1), (1, 0)])
+    partial = pairs(core, mine, other, plane.reshape(64, BINS), table)
     parts = lax.all_to_all(partial.reshape(16, 32, LAGS), ("x", "y"), 0, 0, tiled=True)
     group = lax.axis_index(WIN).astype(jnp.int32).reshape(1)
     return finish(group, block_mask, parts.reshape(512, LAGS))

time: 77.5 us -> 72.8 us (0.939)
  the two profiles are of different devices: /device:TPU:8 before, /device:TPU:1 now
where the time goes in v3:
time: 72.8 us; the launch traced here: 72.3 us
  blocking collectives  32 us (44%)
  starting transfers between devices  19.1 us (26%)
  waiting for transfers between devices  13.5 us (19%)
  Pallas kernels  6.82 us (9%)
  local copies, waits for them, and re-layouts  0.74 us (1%)
    all_gather x1, blocking collectives, shards(): column = lax.all_gather(white, ('zh', 'zl'))  32 us
    ppermute x1, starting transfers between devices, shards(): other = lax.ppermute(mine, 'core', [(0, 1), (1, 0)])  10.2 us
    all_to_all x1, waiting for transfers between devices, shards(): lax.all_to_all(partial.reshape(16, 32, LAGS), ('x', 'y'), 0, 0, tiled=True)  7.31 us
    all_to_all x1, waiting for transfers between devices, shards(): plane = lax.all_to_all(copies, 'x', 0, 0, tiled=True)  6.22 us
    all_to_all x1, starting transfers between devices, shards(): lax.all_to_all(partial.reshape(16, 32, LAGS), ('x', 'y'), 0, 0, tiled=True)  4.91 us
    all_to_all x1, starting transfers between devices, shards(): plane = lax.all_to_all(copies, 'x', 0, 0, tiled=True)  4.02 us
    pallas_call x1, Pallas kernels, pairs(): pl.pallas_call(pair_kernel, out_shape=jax.ShapeDtypeStruct((512, LAGS), j...  3.86 us
    pallas_call x1, Pallas kernels, whiten(): pl.pallas_call(whiten_kernel, out_shape=jax.ShapeDtypeStruct((8, BINS), j...  1.65 us
  transfers between devices with their start and end apart: 3, of which 2 were waited for; matrix products, arithmetic and copies ran while one was open for 0% of the time, Pallas kernels for 0%

profile of v3, /device:TPU:1, one launch (start us, length us, event | category | flops | bytes accessed | tf_op | source)
XLA Modules:
  0.0 72.3 jit_solution(9066649057483510697)
XLA Ops:
  0.0 0.0 copy-start
  0.0 1.6 %shard_map.46 = bf16[8,2048]{1,0:T(8,128)(2,1)} custom-call(s32[1,4]{1,0:T(1,128)} %quality_ref.1, bf16[2,1,4,2048]{3,2,1,0:T(4,128)(2,1)} %spectra_ref.1), custom_call_target="tpu_custom_call" | custom-call | tf_op jit(solution)/shard_map/pallas_call | solution.py:47
  1.6 32.0 %all-gather.column_ref = bf16[128,2048]{1,0:T(8,128)(2,1)S(1)} all-gather(bf16[8,2048]{1,0:T(8,128)(2,1)} %shard_map.46), channel_id=2, replica_groups=mesh['zl'=8,'x'=4,'core'=2,'y'=4,'zh'=2] {'zh','zl'}, dimensions={0}, use_global_device_ids=true | all-gather | bytes 557056 | tf_op jit(solution)/shard_map/all_gather | solution.py:190
  33.7 0.7 broadcast_in_dim.8.sent_ref
  34.4 0.1 shard_map.47.mine_ref
  34.5 0.0 copy-start.1
  34.5 10.2 %collective-permute-start = (bf16[64,2048]{1,0:T(8,128)(2,1)S(1)}, bf16[64,2048]{1,0:T(8,128)(2,1)S(1)}, u32[]{:S(2)}, u32[]{:S(2)}) collective-permute-start(bf16[64,2048]{1,0:T(8,128)(2,1)S(1)} %shard_map.47.mine_ref), channel_id=1, source_target_pairs={{0,8},{8,0},{1,9},{9,1},{2,10},{10,2},{3,11},{11,3},{4,12},{12,4},... | collective-permute-start | bytes 786440 | tf_op jit(solution)/shard_map/ppermute | solution.py:198
  44.7 4.0 %all-to-all-start = ((bf16[4,16,2048]{2,1,0:T(8,128)(2,1)}), bf16[4,16,2048]{2,1,0:T(8,128)(2,1)S(1)}, u32[]{:S(2)}, u32[]{:S(2)}) async-start(bf16[4,16,2048]{2,1,0:T(8,128)(2,1)} %broadcast_in_dim.8.sent_ref), calls=%async_computation | async-start | bytes 524288 | tf_op jit(solution)/shard_map/all_to_all | solution.py:194
  48.7 6.2 %all-to-all-done = bf16[4,16,2048]{2,1,0:T(8,128)(2,1)S(1)} async-done(((bf16[4,16,2048]{2,1,0:T(8,128)(2,1)}), bf16[4,16,2048]{2,1,0:T(8,128)(2,1)S(1)}, u32[]{:S(2)}, u32[]{:S(2)}) %all-to-all-start) | async-done | bytes 262176 | tf_op jit(solution)/shard_map/all_to_all | solution.py:194
  54.9 0.0 collective-permute-done.other_ref
  54.9 0.0 copy-done
  54.9 3.9 %shard_map.48 = bf16[512,256]{1,0:T(8,128)(2,1)} custom-call(s32[1]{0:T(128)} %bitcast.1.core_ref, bf16[64,2048]{1,0:T(8,128)(2,1)S(1)} %shard_map.47.mine_ref, bf16[64,2048]{1,0:T(8,128)(2,1)S(1)} %collective-permute-done.other_ref, bf16[64,2048]{1,0:T(8,128)(2,1)S(1)} %bitcast.11, bf16[4096,256]{1,0:T(8,128)(2,1)S(1)} %copy-done), custom_call_target="tpu_custom_call" | custom-call | tf_op jit(solution)/shard_map/pallas_call | solution.py:136
  58.8 4.9 %all-to-all-start.1 = ((bf16[16,32,256]{2,1,0:T(8,128)(2,1)}), bf16[16,32,256]{2,1,0:T(8,128)(2,1)S(1)}, u32[]{:S(2)}, u32[]{:S(2)}) async-start(bf16[16,32,256]{2,1,0:T(8,128)(2,1)} %bitcast.6), calls=%async_computation.1 | async-start | bytes 524288 | tf_op jit(solution)/shard_map/all_to_all | solution.py:200
  63.7 7.3 %all-to-all-done.1 = bf16[16,32,256]{2,1,0:T(8,128)(2,1)S(1)} async-done(((bf16[16,32,256]{2,1,0:T(8,128)(2,1)}), bf16[16,32,256]{2,1,0:T(8,128)(2,1)S(1)}, u32[]{:S(2)}, u32[]{:S(2)}) %all-to-all-start.1) | async-done | bytes 262176 | tf_op jit(solution)/shard_map/all_to_all | solution.py:200
  71.0 0.0 copy-done.1
  71.1 1.2 %shard_map.49 = bf16[4,32,256]{2,1,0:T(8,128)(2,1)} custom-call(s32[1]{0:T(128)} %bitcast.group_ref, s32[1,64]{1,0:T(1,128)S(1)} %copy-done.1, bf16[512,256]{1,0:T(8,128)(2,1)S(1)} %bitcast.10), custom_call_target="tpu_custom_call" | custom-call | tf_op jit(solution)/shard_map/pallas_call | solution.py:179
  (1 shorter events, 0.0 us)
Async XLA Ops:
  0.0 54.9 %copy-start = (bf16[4096,256]{1,0:T(8,128)(2,1)S(1)}, bf16[4096,256]{1,0:T(8,128)(2,1)}, u32[]{:S(2)}) copy-start(bf16[4096,256]{1,0:T(8,128)(2,1)} %constant.24.clone.table_hbm) | copy-start | bytes 6291460
  34.5 36.5 %copy-start.1 = (s32[1,64]{1,0:T(1,128)S(1)}, s32[1,64]{1,0:T(1,128)}, u32[]{:S(2)}) copy-start(s32[1,64]{1,0:T(1,128)} %mask_ref.1) | copy-start | bytes 772
  34.5 20.4 %collective-permute-start = (bf16[64,2048]{1,0:T(8,128)(2,1)S(1)}, bf16[64,2048]{1,0:T(8,128)(2,1)S(1)}, u32[]{:S(2)}, u32[]{:S(2)}) collective-permute-start(bf16[64,2048]{1,0:T(8,128)(2,1)S(1)} %shard_map.47.mine_ref), channel_id=1, source_target_pairs={{0,8},{8,0},{1,9},{9,1},{2,10},{10,2},{3,11},{11,3},{4,12},{12,4},... | collective-permute-start | bytes 786440 | tf_op jit(solution)/shard_map/ppermute | solution.py:198
  44.7 10.2 %all-to-all-start = ((bf16[4,16,2048]{2,1,0:T(8,128)(2,1)}), bf16[4,16,2048]{2,1,0:T(8,128)(2,1)S(1)}, u32[]{:S(2)}, u32[]{:S(2)}) async-start(bf16[4,16,2048]{2,1,0:T(8,128)(2,1)} %broadcast_in_dim.8.sent_ref), calls=%async_computation | async-start | bytes 524288 | tf_op jit(solution)/shard_map/all_to_all | solution.py:194
  58.8 12.2 %all-to-all-start.1 = ((bf16[16,32,256]{2,1,0:T(8,128)(2,1)}), bf16[16,32,256]{2,1,0:T(8,128)(2,1)S(1)}, u32[]{:S(2)}, u32[]{:S(2)}) async-start(bf16[16,32,256]{2,1,0:T(8,128)(2,1)} %bitcast.6), calls=%async_computation.1 | async-start | bytes 524288 | tf_op jit(solution)/shard_map/all_to_all | solution.py:200

commit v4 on v3

--- a/solution.py
+++ b/solution.py
@@ -74,16 +74,7 @@
     )(half, column, sent)
 
 
-def pair_kernel(
-    core_ref, mine_ref, other_ref, own_ref, table_hbm, out_ref,
-    far, own, cross_even, cross_odd, total, order, table, arrived,
-):
-    fetch = pltpu.make_async_copy(table_hbm, table, arrived)
-    fetch.start()
-    core = core_ref[0]
-    far[core] = mine_ref[...].astype(jnp.float32)
-    far[1 - core] = other_ref[...].astype(jnp.float32)
-    own[...] = own_ref[...].astype(jnp.float32)
+def correlate(stations, far, own, crosses, total, table, ready):
     total[...] = jnp.zeros_like(total)
 
     def products(c, cross):
@@ -91,7 +82,7 @@
         for side in range(2):
             b_re = [far[side, 32 * w : 32 * w + 16, bins] for w in range(2)]
             b_im = [far[side, 32 * w + 16 : 32 * w + 32, bins] for w in range(2)]
-            for i in range(16):
+            for i in range(stations):
                 re, im = None, None
                 for w in range(2):
                     at = (i // 4) * 16 + w * 8 + i % 4
@@ -101,7 +92,7 @@
                     im_w = a_im * b_re[w] - a_re * b_im[w]
                     re = re_w if re is None else re + re_w
                     im = im_w if im is None else im + im_w
-                to = side * 256 + i * 16
+                to = (side * stations + i) * 16
                 cross[to : to + 16, 0:CHUNK] = re.astype(jnp.bfloat16)
                 cross[to : to + 16, CHUNK : 2 * CHUNK] = im.astype(jnp.bfloat16)
 
@@ -109,47 +100,89 @@
         rows = pl.ds(pl.multiple_of(c * 2 * CHUNK, 2 * CHUNK), 2 * CHUNK)
         total[...] += jnp.dot(cross[...], table[rows, :], preferred_element_type=jnp.float32)
 
-    products(0, cross_even)
-    fetch.wait()
+    even, odd = crosses
+    products(0, even)
+    ready()
 
     @pl.loop(0, CHUNKS // 2 - 1)
     def _(c):
-        products(2 * c + 1, cross_odd)
-        to_lags(2 * c, cross_even)
-        products(2 * c + 2, cross_even)
-        to_lags(2 * c + 1, cross_odd)
-
-    products(CHUNKS - 1, cross_odd)
-    to_lags(CHUNKS - 2, cross_even)
-    to_lags(CHUNKS - 1, cross_odd)
-
+        products(2 * c + 1, odd)
+        to_lags(2 * c, even)
+        products(2 * c + 2, even)
+        to_lags(2 * c + 1, odd)
+
+    products(CHUNKS - 1, odd)
+    to_lags(CHUNKS - 2, even)
+    to_lags(CHUNKS - 1, odd)
+
+
+def reorder(stations, total, order):
     for side in range(2):
-        for i in range(16):
-            rows = total[side * 256 + i * 16 : side * 256 + i * 16 + 16, :]
+        for i in range(stations):
+            first = (side * stations + i) * 16
+            rows = total[first : first + 16, :]
             for k in range(4):
                 to = ((i // 4) * 4 + k) * 32 + (i % 4) * 8 + side * 4
                 order[to : to + 4, :] = rows[4 * k : 4 * k + 4]
+
+
+def own_pairs_kernel(
+    far_ref, own_ref, table_hbm, out_ref,
+    far, own, even, odd, total, order, table, arrived,
+):
+    fetch = pltpu.make_async_copy(table_hbm, table, arrived)
+    fetch.start()
+    far[...] = far_ref[...].astype(jnp.float32)
+    own[...] = own_ref[...].astype(jnp.float32)
+    correlate(4, far, own, (even, odd), total, table, fetch.wait)
+    reorder(4, total, order)
     out_ref[...] = order[...].astype(jnp.bfloat16)
 
 
-def pairs(core, mine, other, own, table):
-    return pl.pallas_call(
-        pair_kernel,
-        out_shape=jax.ShapeDtypeStruct((512, LAGS), jnp.bfloat16),
-        in_specs=[SMEM, VMEM, VMEM, VMEM, pl.BlockSpec(memory_space=pl.ANY)],
+def plane_pairs_kernel(
+    x_ref, far_ref, plane_ref, own_part_ref, table_hbm, out_ref,
+    far, own, even, odd, total, order, table, arrived,
+):
+    fetch = pltpu.make_async_copy(table_hbm, table, arrived)
+    fetch.start()
+    far[...] = far_ref[...].astype(jnp.float32)
+    x = x_ref[0]
+    for n in range(3):
+        block = lax.rem(x + n + 1, 4)
+        own[16 * n : 16 * n + 16, :] = plane_ref[pl.ds(pl.multiple_of(block * 16, 16), 16), :].astype(jnp.float32)
+    out_ref[pl.ds(pl.multiple_of(x * 128, 128), 128), :] = own_part_ref[...]
+    correlate(12, far, own, (even, odd), total, table, fetch.wait)
+    reorder(12, total, order)
+    for n in range(3):
+        block = lax.rem(x + n + 1, 4)
+        rows = order[128 * n : 128 * n + 128, :].astype(jnp.bfloat16)
+        out_ref[pl.ds(pl.multiple_of(block * 128, 128), 128), :] = rows
+
+
+def pairs(kernel, blocks, result_rows, *operands):
+    rows = blocks * 128
+    specs = [SMEM if o.dtype == jnp.int32 else VMEM for o in operands]
+    specs[-1] = pl.BlockSpec(memory_space=pl.ANY)
+    return pl.pallas_call(
+        kernel,
+        out_shape=jax.ShapeDtypeStruct((result_rows, LAGS), jnp.bfloat16),
+        in_specs=specs,
         out_specs=VMEM,
         scratch_shapes=[
             pltpu.VMEM((2, 64, BINS), jnp.float32),
-            pltpu.VMEM((64, BINS), jnp.float32),
-            pltpu.VMEM((512, 2 * CHUNK), jnp.bfloat16),
-            pltpu.VMEM((512, 2 * CHUNK), jnp.bfloat16),
-            pltpu.VMEM((512, LAGS), jnp.float32),
-            pltpu.VMEM((512, LAGS), jnp.float32),
+            pltpu.VMEM((16 * blocks, BINS), jnp.float32),
+            pltpu.VMEM((rows, 2 * CHUNK), jnp.bfloat16),
+            pltpu.VMEM((rows, 2 * CHUNK), jnp.bfloat16),
+            pltpu.VMEM((rows, LAGS), jnp.float32),
+            pltpu.VMEM((rows, LAGS), jnp.float32),
             pltpu.VMEM((2 * BINS, LAGS), jnp.bfloat16),
             pltpu.SemaphoreType.DMA,
         ],
         compiler_params=pltpu.CompilerParams(vmem_limit_bytes=40 * 1024 * 1024),
-    )(core, mine, other, own, table)
+        cost_estimate=pl.CostEstimate(
+            flops=4 * rows * BINS * LAGS, bytes_accessed=6 * 2**20, transcendentals=0
+        ),
+    )(*operands)
 
 
 def finish_kernel(group_ref, mask_ref, parts_ref, out_ref):
@@ -193,10 +226,13 @@
     copies = jnp.broadcast_to(own.reshape(1, 16, BINS), (4, 16, BINS))
     plane = lax.all_to_all(copies, "x", 0, 0, tiled=True)
     half = lax.axis_index("zh").astype(jnp.int32).reshape(1)
-    core = lax.axis_index("core").astype(jnp.int32).reshape(1)
     mine = choose(half, column.reshape(128, BINS), copies)
-    other = lax.ppermute(mine, "core", [(0, 1), (1, 0)])
-    partial = pairs(core, mine, other, plane.reshape(64, BINS), table)
+    far = lax.all_gather(mine, "core")
+    x = lax.axis_index("x").astype(jnp.int32).reshape(1)
+    own_part = pairs(own_pairs_kernel, 1, 128, far, own.reshape(16, BINS), table)
+    partial = pairs(
+        plane_pairs_kernel, 3, 512, x, far, plane.reshape(64, BINS), own_part, table
+    )
     parts = lax.all_to_all(partial.reshape(16, 32, LAGS), ("x", "y"), 0, 0, tiled=True)
     group = lax.axis_index(WIN).astype(jnp.int32).reshape(1)
     return finish(group, block_mask, parts.reshape(512, LAGS))

time: 72.8 us -> 69.8 us (0.959)
  blocking collectives: 32 us -> 42.4 us
  starting transfers between devices: 19.1 us -> 11.3 us
  waiting for transfers between devices: 13.5 us -> 7.41 us
  Pallas kernels: 6.82 us -> 7.68 us
    all_gather x0 -> x1, blocking collectives: none -> 10.3 us  [shards(): far = lax.all_gather(mine, 'core')]
    ppermute x1 -> x0, starting transfers between devices: 10.2 us -> none  [shards(): other = lax.ppermute(mine, 'core', [(0, 1), (1, 0)])]
    all_to_all x1, waiting for transfers between devices: 6.22 us -> 0.01 us  [shards(): plane = lax.all_to_all(copies, 'x', 0, 0, tiled=True)]
    all_to_all x1, starting transfers between devices: 4.91 us -> 7.27 us  [shards(): lax.all_to_all(partial.reshape(16, 32, LAGS), ('x', 'y'), 0, 0, tiled=True)]
    pallas_call x1 -> x2, Pallas kernels: 3.86 us -> 4.73 us  [pairs(): pl.pallas_call(kernel, out_shape=jax.ShapeDtypeStruct((result_rows, LAGS)...]
  transfers between devices with their start and end apart: 3 -> 2, of which waited for: 2 -> 1; matrix products, arithmetic and copies ran while one was open for 0% -> 0% of each run, Pallas kernels for 0% -> 2%
where the time goes in v4:
time: 69.8 us; the launch traced here: 69.5 us
  blocking collectives  42.4 us (61%)
  starting transfers between devices  11.3 us (16%)
  Pallas kernels  7.68 us (11%)
  waiting for transfers between devices  7.41 us (11%)
  local copies, waits for them, and re-layouts  0.73 us (1%)
    all_gather x1, blocking collectives, shards(): column = lax.all_gather(white, ('zh', 'zl'))  32 us
    all_gather x1, blocking collectives, shards(): far = lax.all_gather(mine, 'core')  10.3 us
    all_to_all x1, waiting for transfers between devices, shards(): lax.all_to_all(partial.reshape(16, 32, LAGS), ('x', 'y'), 0, 0, tiled=True)  7.41 us
    all_to_all x1, starting transfers between devices, shards(): lax.all_to_all(partial.reshape(16, 32, LAGS), ('x', 'y'), 0, 0, tiled=True)  7.27 us
    pallas_call x2, Pallas kernels, pairs(): pl.pallas_call(kernel, out_shape=jax.ShapeDtypeStruct((result_rows, LAGS)...  4.73 us
    all_to_all x1, starting transfers between devices, shards(): plane = lax.all_to_all(copies, 'x', 0, 0, tiled=True)  4.01 us
    pallas_call x1, Pallas kernels, whiten(): pl.pallas_call(whiten_kernel, out_shape=jax.ShapeDtypeStruct((8, BINS), j...  1.65 us
  transfers between devices with their start and end apart: 2, of which 1 were waited for; matrix products, arithmetic and copies ran while one was open for 0% of the time, Pallas kernels for 2%

profile of v4, /device:TPU:1, one launch (start us, length us, event | category | flops | bytes accessed | tf_op | source)
XLA Modules:
  0.0 69.5 jit_solution(623931225791761302)
XLA Ops:
  0.0 0.0 copy-start
  0.0 1.6 %shard_map.46 = bf16[8,2048]{1,0:T(8,128)(2,1)} custom-call(s32[1,4]{1,0:T(1,128)} %quality_ref.1, bf16[2,1,4,2048]{3,2,1,0:T(4,128)(2,1)} %spectra_ref.1), custom_call_target="tpu_custom_call" | custom-call | tf_op jit(solution)/shard_map/pallas_call | solution.py:47
  1.6 32.0 %all-gather.column_ref = bf16[128,2048]{1,0:T(8,128)(2,1)S(1)} all-gather(bf16[8,2048]{1,0:T(8,128)(2,1)} %shard_map.46), channel_id=2, replica_groups=mesh['zl'=8,'x'=4,'core'=2,'y'=4,'zh'=2] {'zh','zl'}, dimensions={0}, use_global_device_ids=true | all-gather | bytes 557056 | tf_op jit(solution)/shard_map/all_gather | solution.py:223
  33.7 0.7 %broadcast_in_dim.8.sent_ref = bf16[4,16,2048]{2,1,0:T(8,128)(2,1)} broadcast(bf16[16,2048]{1,0:T(8,128)(2,1)S(1)} %dynamic-slice_bitcast_fusion.own_ref), dimensions={1,2} | broadcast | bytes 327680 | tf_op jit(solution)/shard_map/broadcast_in_dim | solution.py:226
  34.4 4.0 %all-to-all-start = ((bf16[4,16,2048]{2,1,0:T(8,128)(2,1)}), bf16[4,16,2048]{2,1,0:T(8,128)(2,1)S(1)}, u32[]{:S(2)}, u32[]{:S(2)}) async-start(bf16[4,16,2048]{2,1,0:T(8,128)(2,1)} %broadcast_in_dim.8.sent_ref), calls=%async_computation | async-start | bytes 524288 | tf_op jit(solution)/shard_map/all_to_all | solution.py:227
  38.4 0.1 shard_map.47
  38.5 10.3 %all-gather.1 = bf16[128,2048]{1,0:T(8,128)(2,1)S(1)} all-gather(bf16[64,2048]{1,0:T(8,128)(2,1)S(1)} %shard_map.47), channel_id=3, replica_groups=mesh['zl'=8,'x'=4,'core'=2,'y'=4,'zh'=2] {'core'}, dimensions={0}, use_global_device_ids=true | all-gather | bytes 786432 | tf_op jit(solution)/shard_map/all_gather | solution.py:230
  48.9 0.0 copy-done
  48.9 1.5 %shard_map.48.own_part_ref = bf16[128,256]{1,0:T(8,128)(2,1)S(1)} custom-call(bf16[2,64,2048]{2,1,0:T(8,128)(2,1)S(1)} %bitcast.12, bf16[16,2048]{1,0:T(8,128)(2,1)S(1)} %dynamic-slice_bitcast_fusion.own_ref, bf16[4096,256]{1,0:T(8,128)(2,1)S(1)} %copy-done), custom_call_target="tpu_custom_call" | custom-call | flops 268435456 | bytes 6291456 | tf_op jit(solution)/shard_map/pallas_call | solution.py:166
  50.3 0.0 copy-start.1
  50.3 0.0 all-to-all-done
  50.4 3.3 %shard_map.49 = bf16[512,256]{1,0:T(8,128)(2,1)} custom-call(s32[1]{0:T(128)} %bitcast.1.x_ref, bf16[2,64,2048]{2,1,0:T(8,128)(2,1)S(1)} %bitcast.13, bf16[64,2048]{1,0:T(8,128)(2,1)S(1)} %bitcast.16, bf16[128,256]{1,0:T(8,128)(2,1)S(1)} %shard_map.48.own_part_ref, bf16[4096,256]{1,0:T(8,128)(2,1)S(1)} %copy-done), custom_call_target="tpu_custom_call" | custom-call | flops 805306368 | bytes 6291456 | tf_op jit(solution)/shard_map/pallas_call | solution.py:166
  53.6 7.3 %all-to-all-start.1 = ((bf16[16,32,256]{2,1,0:T(8,128)(2,1)}), bf16[16,32,256]{2,1,0:T(8,128)(2,1)S(1)}, u32[]{:S(2)}, u32[]{:S(2)}) async-start(bf16[16,32,256]{2,1,0:T(8,128)(2,1)} %bitcast.7), calls=%async_computation.1 | async-start | bytes 524288 | tf_op jit(solution)/shard_map/all_to_all | solution.py:236
  60.9 7.4 %all-to-all-done.1 = bf16[16,32,256]{2,1,0:T(8,128)(2,1)S(1)} async-done(((bf16[16,32,256]{2,1,0:T(8,128)(2,1)}), bf16[16,32,256]{2,1,0:T(8,128)(2,1)S(1)}, u32[]{:S(2)}, u32[]{:S(2)}) %all-to-all-start.1) | async-done | bytes 262176 | tf_op jit(solution)/shard_map/all_to_all | solution.py:236
  68.3 0.0 copy-done.1
  68.3 1.2 %shard_map.50 = bf16[4,32,256]{2,1,0:T(8,128)(2,1)} custom-call(s32[1]{0:T(128)} %bitcast.group_ref, s32[1,64]{1,0:T(1,128)S(1)} %copy-done.1, bf16[512,256]{1,0:T(8,128)(2,1)S(1)} %bitcast.15), custom_call_target="tpu_custom_call" | custom-call | tf_op jit(solution)/shard_map/pallas_call | solution.py:212
  (1 shorter events, 0.0 us)
Async XLA Ops:
  0.0 48.9 %copy-start = (bf16[4096,256]{1,0:T(8,128)(2,1)S(1)}, bf16[4096,256]{1,0:T(8,128)(2,1)}, u32[]{:S(2)}) copy-start(bf16[4096,256]{1,0:T(8,128)(2,1)} %constant.26.clone.table_hbm) | copy-start | bytes 6291460
  34.4 15.9 %all-to-all-start = ((bf16[4,16,2048]{2,1,0:T(8,128)(2,1)}), bf16[4,16,2048]{2,1,0:T(8,128)(2,1)S(1)}, u32[]{:S(2)}, u32[]{:S(2)}) async-start(bf16[4,16,2048]{2,1,0:T(8,128)(2,1)} %broadcast_in_dim.8.sent_ref), calls=%async_computation | async-start | bytes 524288 | tf_op jit(solution)/shard_map/all_to_all | solution.py:227
  50.3 18.0 %copy-start.1 = (s32[1,64]{1,0:T(1,128)S(1)}, s32[1,64]{1,0:T(1,128)}, u32[]{:S(2)}) copy-start(s32[1,64]{1,0:T(1,128)} %mask_ref.1) | copy-start | bytes 772
  53.6 14.7 %all-to-all-start.1 = ((bf16[16,32,256]{2,1,0:T(8,128)(2,1)}), bf16[16,32,256]{2,1,0:T(8,128)(2,1)S(1)}, u32[]{:S(2)}, u32[]{:S(2)}) async-start(bf16[16,32,256]{2,1,0:T(8,128)(2,1)} %bitcast.7), calls=%async_computation.1 | async-start | bytes 524288 | tf_op jit(solution)/shard_map/all_to_all | solution.py:236

commit v5 on v4

--- a/solution.py
+++ b/solution.py
@@ -14,6 +14,8 @@
 BINS = 2048
 CHUNK = 256
 CHUNKS = BINS // CHUNK
+STEP = 2
+STEPS = CHUNKS // STEP
 GRID = (("zl", 8), ("x", 4), ("core", 2), ("y", 4), ("zh", 2))
 STA = ("zl", "x", "core")
 WIN = ("y", "zh")
@@ -74,46 +76,47 @@
     )(half, column, sent)
 
 
-def correlate(stations, far, own, crosses, total, table, ready):
+def correlate(stations, far, own, crosses, total, table):
     total[...] = jnp.zeros_like(total)
 
-    def products(c, cross):
-        bins = pl.ds(pl.multiple_of(c * CHUNK, CHUNK), CHUNK)
-        for side in range(2):
-            b_re = [far[side, 32 * w : 32 * w + 16, bins] for w in range(2)]
-            b_im = [far[side, 32 * w + 16 : 32 * w + 32, bins] for w in range(2)]
-            for i in range(stations):
-                re, im = None, None
-                for w in range(2):
-                    at = (i // 4) * 16 + w * 8 + i % 4
-                    a_re = own[at : at + 1, bins]
-                    a_im = own[at + 4 : at + 5, bins]
-                    re_w = a_re * b_re[w] + a_im * b_im[w]
-                    im_w = a_im * b_re[w] - a_re * b_im[w]
-                    re = re_w if re is None else re + re_w
-                    im = im_w if im is None else im + im_w
-                to = (side * stations + i) * 16
-                cross[to : to + 16, 0:CHUNK] = re.astype(jnp.bfloat16)
-                cross[to : to + 16, CHUNK : 2 * CHUNK] = im.astype(jnp.bfloat16)
-
-    def to_lags(c, cross):
-        rows = pl.ds(pl.multiple_of(c * 2 * CHUNK, 2 * CHUNK), 2 * CHUNK)
+    def products(step, cross):
+        for part in range(STEP):
+            bins = pl.ds(pl.multiple_of((step * STEP + part) * CHUNK, CHUNK), CHUNK)
+            for side in range(2):
+                b_re = [far[side, 32 * w : 32 * w + 16, bins] for w in range(2)]
+                b_im = [far[side, 32 * w + 16 : 32 * w + 32, bins] for w in range(2)]
+                for i in range(stations):
+                    re, im = None, None
+                    for w in range(2):
+                        at = (i // 4) * 16 + w * 8 + i % 4
+                        a_re = own[at : at + 1, bins]
+                        a_im = own[at + 4 : at + 5, bins]
+                        re_w = a_re * b_re[w] + a_im * b_im[w]
+                        im_w = a_im * b_re[w] - a_re * b_im[w]
+                        re = re_w if re is None else re + re_w
+                        im = im_w if im is None else im + im_w
+                    to, first = (side * stations + i) * 16, 2 * CHUNK * part
+                    cross[to : to + 16, first : first + CHUNK] = re.astype(jnp.bfloat16)
+                    cross[to : to + 16, first + CHUNK : first + 2 * CHUNK] = im.astype(jnp.bfloat16)
+
+    def to_lags(step, cross):
+        depth = 2 * CHUNK * STEP
+        rows = pl.ds(pl.multiple_of(step * depth, depth), depth)
         total[...] += jnp.dot(cross[...], table[rows, :], preferred_element_type=jnp.float32)
 
     even, odd = crosses
     products(0, even)
-    ready()
-
-    @pl.loop(0, CHUNKS // 2 - 1)
-    def _(c):
-        products(2 * c + 1, odd)
-        to_lags(2 * c, even)
-        products(2 * c + 2, even)
-        to_lags(2 * c + 1, odd)
-
-    products(CHUNKS - 1, odd)
-    to_lags(CHUNKS - 2, even)
-    to_lags(CHUNKS - 1, odd)
+
+    @pl.loop(0, STEPS // 2 - 1)
+    def _(n):
+        products(2 * n + 1, odd)
+        to_lags(2 * n, even)
+        products(2 * n + 2, even)
+        to_lags(2 * n + 1, odd)
+
+    products(STEPS - 1, odd)
+    to_lags(STEPS - 2, even)
+    to_lags(STEPS - 1, odd)
 
 
 def reorder(stations, total, order):
@@ -127,31 +130,27 @@
 
 
 def own_pairs_kernel(
-    far_ref, own_ref, table_hbm, out_ref,
-    far, own, even, odd, total, order, table, arrived,
+    far_ref, own_ref, table, out_ref,
+    far, own, even, odd, total, order,
 ):
-    fetch = pltpu.make_async_copy(table_hbm, table, arrived)
-    fetch.start()
     far[...] = far_ref[...].astype(jnp.float32)
     own[...] = own_ref[...].astype(jnp.float32)
-    correlate(4, far, own, (even, odd), total, table, fetch.wait)
+    correlate(4, far, own, (even, odd), total, table)
     reorder(4, total, order)
     out_ref[...] = order[...].astype(jnp.bfloat16)
 
 
 def plane_pairs_kernel(
-    x_ref, far_ref, plane_ref, own_part_ref, table_hbm, out_ref,
-    far, own, even, odd, total, order, table, arrived,
+    x_ref, far_ref, plane_ref, own_part_ref, table, out_ref,
+    far, own, even, odd, total, order,
 ):
-    fetch = pltpu.make_async_copy(table_hbm, table, arrived)
-    fetch.start()
     far[...] = far_ref[...].astype(jnp.float32)
     x = x_ref[0]
     for n in range(3):
         block = lax.rem(x + n + 1, 4)
         own[16 * n : 16 * n + 16, :] = plane_ref[pl.ds(pl.multiple_of(block * 16, 16), 16), :].astype(jnp.float32)
     out_ref[pl.ds(pl.multiple_of(x * 128, 128), 128), :] = own_part_ref[...]
-    correlate(12, far, own, (even, odd), total, table, fetch.wait)
+    correlate(12, far, own, (even, odd), total, table)
     reorder(12, total, order)
     for n in range(3):
         block = lax.rem(x + n + 1, 4)
@@ -162,7 +161,6 @@
 def pairs(kernel, blocks, result_rows, *operands):
     rows = blocks * 128
     specs = [SMEM if o.dtype == jnp.int32 else VMEM for o in operands]
-    specs[-1] = pl.BlockSpec(memory_space=pl.ANY)
     return pl.pallas_call(
         kernel,
         out_shape=jax.ShapeDtypeStruct((result_rows, LAGS), jnp.bfloat16),
@@ -171,12 +169,10 @@
         scratch_shapes=[
             pltpu.VMEM((2, 64, BINS), jnp.float32),
             pltpu.VMEM((16 * blocks, BINS), jnp.float32),
-            pltpu.VMEM((rows, 2 * CHUNK), jnp.bfloat16),
-            pltpu.VMEM((rows, 2 * CHUNK), jnp.bfloat16),
+            pltpu.VMEM((rows, 2 * CHUNK * STEP), jnp.bfloat16),
+            pltpu.VMEM((rows, 2 * CHUNK * STEP), jnp.bfloat16),
             pltpu.VMEM((rows, LAGS), jnp.float32),
             pltpu.VMEM((rows, LAGS), jnp.float32),
-            pltpu.VMEM((2 * BINS, LAGS), jnp.bfloat16),
-            pltpu.SemaphoreType.DMA,
         ],
         compiler_params=pltpu.CompilerParams(vmem_limit_bytes=40 * 1024 * 1024),
         cost_estimate=pl.CostEstimate(

time: 69.8 us -> 68.6 us (0.983)
  Pallas kernels: 7.68 us -> 6.25 us
    pallas_call x2, Pallas kernels: 4.73 us -> 3.3 us  [pairs(): pl.pallas_call(kernel, out_shape=jax.ShapeDtypeStruct((result_rows, LAGS)...]
  transfers between devices with their start and end apart: 2 -> 2, of which waited for: 1 -> 1; matrix products, arithmetic and copies ran while one was open for 0% -> 0% of each run, Pallas kernels for 2% -> 1%
where the time goes in v5:
time: 68.6 us; the launch traced here: 68 us
  blocking collectives  42.4 us (62%)
  starting transfers between devices  11.3 us (16%)
  waiting for transfers between devices  7.32 us (11%)
  Pallas kernels  6.25 us (9%)
  local copies, waits for them, and re-layouts  0.73 us (1%)
    all_gather x1, blocking collectives, shards(): column = lax.all_gather(white, ('zh', 'zl'))  32 us
    all_gather x1, blocking collectives, shards(): far = lax.all_gather(mine, 'core')  10.3 us
    all_to_all x1, waiting for transfers between devices, shards(): lax.all_to_all(partial.reshape(16, 32, LAGS), ('x', 'y'), 0, 0, tiled=True)  7.31 us
    all_to_all x1, starting transfers between devices, shards(): lax.all_to_all(partial.reshape(16, 32, LAGS), ('x', 'y'), 0, 0, tiled=True)  7.26 us
    all_to_all x1, starting transfers between devices, shards(): plane = lax.all_to_all(copies, 'x', 0, 0, tiled=True)  4.01 us
    pallas_call x2, Pallas kernels, pairs(): pl.pallas_call(kernel, out_shape=jax.ShapeDtypeStruct((result_rows, LAGS)...  3.3 us
    pallas_call x1, Pallas kernels, whiten(): pl.pallas_call(whiten_kernel, out_shape=jax.ShapeDtypeStruct((8, BINS), j...  1.65 us
  transfers between devices with their start and end apart: 2, of which 1 were waited for; matrix products, arithmetic and copies ran while one was open for 0% of the time, Pallas kernels for 1%

profile of v5, /device:TPU:1, one launch (start us, length us, event | category | flops | bytes accessed | tf_op | source)
XLA Modules:
  0.0 68.0 jit_solution(7568008447218401951)
XLA Ops:
  0.0 0.0 copy-start
  0.0 1.6 %shard_map.46 = bf16[8,2048]{1,0:T(8,128)(2,1)} custom-call(s32[1,4]{1,0:T(1,128)} %quality_ref.1, bf16[2,1,4,2048]{3,2,1,0:T(4,128)(2,1)} %spectra_ref.1), custom_call_target="tpu_custom_call" | custom-call | tf_op jit(solution)/shard_map/pallas_call | solution.py:49
  1.6 32.0 %all-gather.column_ref = bf16[128,2048]{1,0:T(8,128)(2,1)S(1)} all-gather(bf16[8,2048]{1,0:T(8,128)(2,1)} %shard_map.46), channel_id=2, replica_groups=mesh['zl'=8,'x'=4,'core'=2,'y'=4,'zh'=2] {'zh','zl'}, dimensions={0}, use_global_device_ids=true | all-gather | bytes 557056 | tf_op jit(solution)/shard_map/all_gather | solution.py:219
  33.7 0.7 %broadcast_in_dim.8.sent_ref = bf16[4,16,2048]{2,1,0:T(8,128)(2,1)} broadcast(bf16[16,2048]{1,0:T(8,128)(2,1)S(1)} %dynamic-slice_bitcast_fusion.own_ref), dimensions={1,2} | broadcast | bytes 327680 | tf_op jit(solution)/shard_map/broadcast_in_dim | solution.py:222
  34.4 4.0 %all-to-all-start = ((bf16[4,16,2048]{2,1,0:T(8,128)(2,1)}), bf16[4,16,2048]{2,1,0:T(8,128)(2,1)S(1)}, u32[]{:S(2)}, u32[]{:S(2)}) async-start(bf16[4,16,2048]{2,1,0:T(8,128)(2,1)} %broadcast_in_dim.8.sent_ref), calls=%async_computation | async-start | bytes 524288 | tf_op jit(solution)/shard_map/all_to_all | solution.py:223
  38.4 0.1 shard_map.47
  38.5 10.3 %all-gather.1 = bf16[128,2048]{1,0:T(8,128)(2,1)S(1)} all-gather(bf16[64,2048]{1,0:T(8,128)(2,1)S(1)} %shard_map.47), channel_id=3, replica_groups=mesh['zl'=8,'x'=4,'core'=2,'y'=4,'zh'=2] {'core'}, dimensions={0}, use_global_device_ids=true | all-gather | bytes 786432 | tf_op jit(solution)/shard_map/all_gather | solution.py:226
  48.9 0.0 copy-done
  48.9 0.8 %shard_map.48.own_part_ref = bf16[128,256]{1,0:T(8,128)(2,1)S(1)} custom-call(bf16[2,64,2048]{2,1,0:T(8,128)(2,1)S(1)} %bitcast.12, bf16[16,2048]{1,0:T(8,128)(2,1)S(1)} %dynamic-slice_bitcast_fusion.own_ref, bf16[4096,256]{1,0:T(8,128)(2,1)S(1)} %copy-done), custom_call_target="tpu_custom_call" | custom-call | flops 268435456 | bytes 6291456 | tf_op jit(solution)/shard_map/pallas_call | solution.py:164
  49.7 0.0 copy-start.1
  49.7 0.0 all-to-all-done
  49.7 2.5 %shard_map.49 = bf16[512,256]{1,0:T(8,128)(2,1)} custom-call(s32[1]{0:T(128)} %bitcast.1.x_ref, bf16[2,64,2048]{2,1,0:T(8,128)(2,1)S(1)} %bitcast.13, bf16[64,2048]{1,0:T(8,128)(2,1)S(1)} %bitcast.16, bf16[128,256]{1,0:T(8,128)(2,1)S(1)} %shard_map.48.own_part_ref, bf16[4096,256]{1,0:T(8,128)(2,1)S(1)} %copy-done), custom_call_target="tpu_custom_call" | custom-call | flops 805306368 | bytes 6291456 | tf_op jit(solution)/shard_map/pallas_call | solution.py:164
  52.2 7.3 %all-to-all-start.1 = ((bf16[16,32,256]{2,1,0:T(8,128)(2,1)}), bf16[16,32,256]{2,1,0:T(8,128)(2,1)S(1)}, u32[]{:S(2)}, u32[]{:S(2)}) async-start(bf16[16,32,256]{2,1,0:T(8,128)(2,1)} %bitcast.7), calls=%async_computation.1 | async-start | bytes 524288 | tf_op jit(solution)/shard_map/all_to_all | solution.py:232
  59.5 7.3 %all-to-all-done.1 = bf16[16,32,256]{2,1,0:T(8,128)(2,1)S(1)} async-done(((bf16[16,32,256]{2,1,0:T(8,128)(2,1)}), bf16[16,32,256]{2,1,0:T(8,128)(2,1)S(1)}, u32[]{:S(2)}, u32[]{:S(2)}) %all-to-all-start.1) | async-done | bytes 262176 | tf_op jit(solution)/shard_map/all_to_all | solution.py:232
  66.8 0.0 copy-done.1
  66.8 1.2 %shard_map.50 = bf16[4,32,256]{2,1,0:T(8,128)(2,1)} custom-call(s32[1]{0:T(128)} %bitcast.group_ref, s32[1,64]{1,0:T(1,128)S(1)} %copy-done.1, bf16[512,256]{1,0:T(8,128)(2,1)S(1)} %bitcast.15), custom_call_target="tpu_custom_call" | custom-call | tf_op jit(solution)/shard_map/pallas_call | solution.py:208
  (1 shorter events, 0.0 us)
Async XLA Ops:
  0.0 48.9 %copy-start = (bf16[4096,256]{1,0:T(8,128)(2,1)S(1)}, bf16[4096,256]{1,0:T(8,128)(2,1)}, u32[]{:S(2)}) copy-start(bf16[4096,256]{1,0:T(8,128)(2,1)} %constant.26.clone.table) | copy-start | bytes 6291460
  34.4 15.3 %all-to-all-start = ((bf16[4,16,2048]{2,1,0:T(8,128)(2,1)}), bf16[4,16,2048]{2,1,0:T(8,128)(2,1)S(1)}, u32[]{:S(2)}, u32[]{:S(2)}) async-start(bf16[4,16,2048]{2,1,0:T(8,128)(2,1)} %broadcast_in_dim.8.sent_ref), calls=%async_computation | async-start | bytes 524288 | tf_op jit(solution)/shard_map/all_to_all | solution.py:223
  49.7 17.1 %copy-start.1 = (s32[1,64]{1,0:T(1,128)S(1)}, s32[1,64]{1,0:T(1,128)}, u32[]{:S(2)}) copy-start(s32[1,64]{1,0:T(1,128)} %mask_ref.1) | copy-start | bytes 772
  52.2 14.6 %all-to-all-start.1 = ((bf16[16,32,256]{2,1,0:T(8,128)(2,1)}), bf16[16,32,256]{2,1,0:T(8,128)(2,1)S(1)}, u32[]{:S(2)}, u32[]{:S(2)}) async-start(bf16[16,32,256]{2,1,0:T(8,128)(2,1)} %bitcast.7), calls=%async_computation.1 | async-start | bytes 524288 | tf_op jit(solution)/shard_map/all_to_all | solution.py:232

commit v6 on v5

--- a/solution.py
+++ b/solution.py
@@ -54,8 +54,8 @@
     )(quality, spectra)
 
 
-def choose_kernel(half_ref, column_ref, sent_ref, chosen_ref):
-    second = half_ref[0] == 1
+def choose_kernel(column_ref, sent_ref, chosen_ref):
+    second = lax.axis_index("zh") == 1
     for w in range(2):
         parts = []
         for k in range(4):
@@ -66,14 +66,14 @@
             chosen_ref[(w * 2 + c) * 16 : (w * 2 + c) * 16 + 16, :] = rows.astype(jnp.bfloat16)
 
 
-def choose(half, column, sent):
+def choose(column, sent):
     return pl.pallas_call(
         choose_kernel,
         out_shape=jax.ShapeDtypeStruct((64, BINS), jnp.bfloat16),
-        in_specs=[SMEM, VMEM, pl.BlockSpec(memory_space=pl.ANY)],
+        in_specs=[VMEM, pl.BlockSpec(memory_space=pl.ANY)],
         out_specs=VMEM,
         compiler_params=SMALL,
-    )(half, column, sent)
+    )(column, sent)
 
 
 def correlate(stations, far, own, crosses, total, table):
@@ -141,11 +141,11 @@
 
 
 def plane_pairs_kernel(
-    x_ref, far_ref, plane_ref, own_part_ref, table, out_ref,
+    far_ref, plane_ref, own_part_ref, table, out_ref,
     far, own, even, odd, total, order,
 ):
     far[...] = far_ref[...].astype(jnp.float32)
-    x = x_ref[0]
+    x = lax.axis_index("x")
     for n in range(3):
         block = lax.rem(x + n + 1, 4)
         own[16 * n : 16 * n + 16, :] = plane_ref[pl.ds(pl.multiple_of(block * 16, 16), 16), :].astype(jnp.float32)
@@ -160,11 +160,10 @@
 
 def pairs(kernel, blocks, result_rows, *operands):
     rows = blocks * 128
-    specs = [SMEM if o.dtype == jnp.int32 else VMEM for o in operands]
     return pl.pallas_call(
         kernel,
         out_shape=jax.ShapeDtypeStruct((result_rows, LAGS), jnp.bfloat16),
-        in_specs=specs,
+        in_specs=[VMEM] * len(operands),
         out_specs=VMEM,
         scratch_shapes=[
             pltpu.VMEM((2, 64, BINS), jnp.float32),
@@ -181,9 +180,11 @@
     )(*operands)
 
 
-def finish_kernel(group_ref, mask_ref, parts_ref, out_ref):
-    first = group_ref[0] * 8
-    upper = lax.broadcasted_iota(jnp.int32, (8, 1), 0) < 4
+def finish_kernel(mask_ref, parts_ref, out_ref):
+    first = (lax.axis_index("y") * 2 + lax.axis_index("zh")) * 8
+    lane = lax.broadcasted_iota(jnp.int32, (8, 64), 1)
+    core = lax.broadcasted_iota(jnp.int32, (8, 64), 0) // 4
+    flags = jnp.broadcast_to(mask_ref[...].astype(jnp.float32), (8, 64))
     for pair in range(2):
         sums, masks = [], []
         for x in (2 * pair, 2 * pair + 1):
@@ -192,26 +193,21 @@
                 part = parts_ref[(x * 4 + y) * 32 : (x * 4 + y) * 32 + 32, :].astype(jnp.float32)
                 total = part if total is None else total + part
             sums.append(total)
-            masks.append(
-                jnp.where(
-                    upper,
-                    mask_ref[0, first + 2 * x].astype(jnp.float32),
-                    mask_ref[0, first + 2 * x + 1].astype(jnp.float32),
-                )
-            )
+            here = lane == first + 2 * x + core
+            masks.append(jnp.sum(jnp.where(here, flags, 0.0), axis=1, keepdims=True))
         for i in range(4):
             rows = jnp.concatenate([s[8 * i : 8 * i + 8] * m for s, m in zip(sums, masks)], axis=0)
             out_ref[i, 16 * pair : 16 * pair + 16, :] = rows.astype(jnp.bfloat16)
 
 
-def finish(group, block_mask, parts):
+def finish(block_mask, parts):
     return pl.pallas_call(
         finish_kernel,
         out_shape=jax.ShapeDtypeStruct((4, 32, LAGS), jnp.bfloat16),
-        in_specs=[SMEM, SMEM, VMEM],
+        in_specs=[VMEM, VMEM],
         out_specs=VMEM,
         compiler_params=SMALL,
-    )(group, block_mask, parts)
+    )(block_mask, parts)
 
 
 def shards(table, spectra, quality, block_mask):
@@ -221,17 +217,14 @@
     own = lax.dynamic_slice_in_dim(column.reshape(2, 8, 8, BINS), zl, 1, axis=1)
     copies = jnp.broadcast_to(own.reshape(1, 16, BINS), (4, 16, BINS))
     plane = lax.all_to_all(copies, "x", 0, 0, tiled=True)
-    half = lax.axis_index("zh").astype(jnp.int32).reshape(1)
-    mine = choose(half, column.reshape(128, BINS), copies)
+    mine = choose(column.reshape(128, BINS), copies)
     far = lax.all_gather(mine, "core")
-    x = lax.axis_index("x").astype(jnp.int32).reshape(1)
     own_part = pairs(own_pairs_kernel, 1, 128, far, own.reshape(16, BINS), table)
     partial = pairs(
-        plane_pairs_kernel, 3, 512, x, far, plane.reshape(64, BINS), own_part, table
+        plane_pairs_kernel, 3, 512, far, plane.reshape(64, BINS), own_part, table
     )
     parts = lax.all_to_all(partial.reshape(16, 32, LAGS), ("x", "y"), 0, 0, tiled=True)
-    group = lax.axis_index(WIN).astype(jnp.int32).reshape(1)
-    return finish(group, block_mask, parts.reshape(512, LAGS))
+    return finish(block_mask, parts.reshape(512, LAGS))
 
 
 def solution(mesh):

time: 68.6 us -> 67.2 us (0.980)
  blocking collectives: 42.4 us -> 56.8 us
  waiting for transfers between devices: 7.32 us -> 0.01 us
  starting transfers between devices: 11.3 us -> 4.01 us
  Pallas kernels: 6.25 us -> 5.06 us
    all_to_all x0 -> x1, blocking collectives: none -> 14.4 us  [shards(): lax.all_to_all(partial.reshape(16, 32, LAGS), ('x', 'y'), 0, 0, tiled=True)]
    all_to_all x1 -> x0, waiting for transfers between devices: 7.31 us -> none  [shards(): lax.all_to_all(partial.reshape(16, 32, LAGS), ('x', 'y'), 0, 0, tiled=True)]
    all_to_all x1 -> x0, starting transfers between devices: 7.26 us -> none  [shards(): lax.all_to_all(partial.reshape(16, 32, LAGS), ('x', 'y'), 0, 0, tiled=True)]
    pallas_call x2, Pallas kernels: 3.3 us -> 2.59 us  [pairs(): pl.pallas_call(kernel, out_shape=jax.ShapeDtypeStruct((result_rows, LAGS)...]
  transfers between devices with their start and end apart: 2 -> 1, of which waited for: 1 -> 0; matrix products, arithmetic and copies ran while one was open for 0% -> 0% of each run, Pallas kernels for 1% -> 1%
where the time goes in v6:
time: 67.2 us; the launch traced here: 66.6 us
  blocking collectives  56.8 us (85%)
  Pallas kernels  5.06 us (8%)
  starting transfers between devices  4.01 us (6%)
  local copies, waits for them, and re-layouts  0.72 us (1%)
    all_gather x1, blocking collectives, shards(): column = lax.all_gather(white, ('zh', 'zl'))  32 us
    all_to_all x1, blocking collectives, shards(): lax.all_to_all(partial.reshape(16, 32, LAGS), ('x', 'y'), 0, 0, tiled=True)  14.4 us
    all_gather x1, blocking collectives, shards(): far = lax.all_gather(mine, 'core')  10.3 us
    all_to_all x1, starting transfers between devices, shards(): plane = lax.all_to_all(copies, 'x', 0, 0, tiled=True)  4.01 us
    pallas_call x2, Pallas kernels, pairs(): pl.pallas_call(kernel, out_shape=jax.ShapeDtypeStruct((result_rows, LAGS)...  2.59 us
    pallas_call x1, Pallas kernels, whiten(): pl.pallas_call(whiten_kernel, out_shape=jax.ShapeDtypeStruct((8, BINS), j...  1.65 us
  transfers between devices with their start and end apart: 1, of which 0 were waited for; matrix products, arithmetic and copies ran while one was open for 0% of the time, Pallas kernels for 1%

profile of v6, /device:TPU:1, one launch (start us, length us, event | category | flops | bytes accessed | tf_op | source)
XLA Modules:
  0.0 66.6 jit_solution(5945541302204156828)
XLA Ops:
  0.0 0.0 copy-start
  0.0 1.6 %shard_map.46 = bf16[8,2048]{1,0:T(8,128)(2,1)} custom-call(s32[1,4]{1,0:T(1,128)} %quality_ref.1, bf16[2,1,4,2048]{3,2,1,0:T(4,128)(2,1)} %spectra_ref.1), custom_call_target="tpu_custom_call" | custom-call | tf_op jit(solution)/shard_map/pallas_call | solution.py:49
  1.6 32.0 %all-gather.column_ref = bf16[128,2048]{1,0:T(8,128)(2,1)S(1)} all-gather(bf16[8,2048]{1,0:T(8,128)(2,1)} %shard_map.46), channel_id=2, replica_groups=mesh['zl'=8,'x'=4,'core'=2,'y'=4,'zh'=2] {'zh','zl'}, dimensions={0}, use_global_device_ids=true | all-gather | bytes 557056 | tf_op jit(solution)/shard_map/all_gather | solution.py:215
  33.7 0.7 %broadcast_in_dim.8.sent_ref = bf16[4,16,2048]{2,1,0:T(8,128)(2,1)} broadcast(bf16[16,2048]{1,0:T(8,128)(2,1)S(1)} %dynamic-slice_bitcast_fusion.own_ref), dimensions={1,2} | broadcast | bytes 327680 | tf_op jit(solution)/shard_map/broadcast_in_dim | solution.py:218
  34.4 4.0 %all-to-all-start = ((bf16[4,16,2048]{2,1,0:T(8,128)(2,1)}), bf16[4,16,2048]{2,1,0:T(8,128)(2,1)S(1)}, u32[]{:S(2)}, u32[]{:S(2)}) async-start(bf16[4,16,2048]{2,1,0:T(8,128)(2,1)} %broadcast_in_dim.8.sent_ref), calls=%async_computation | async-start | bytes 524288 | tf_op jit(solution)/shard_map/all_to_all | solution.py:219
  38.4 0.1 shard_map.47
  38.5 10.3 %all-gather.1 = bf16[128,2048]{1,0:T(8,128)(2,1)S(1)} all-gather(bf16[64,2048]{1,0:T(8,128)(2,1)S(1)} %shard_map.47), channel_id=3, replica_groups=mesh['zl'=8,'x'=4,'core'=2,'y'=4,'zh'=2] {'core'}, dimensions={0}, use_global_device_ids=true | all-gather | bytes 786432 | tf_op jit(solution)/shard_map/all_gather | solution.py:221
  48.9 0.0 copy-done
  48.9 0.8 %shard_map.48.own_part_ref = bf16[128,256]{1,0:T(8,128)(2,1)S(1)} custom-call(bf16[2,64,2048]{2,1,0:T(8,128)(2,1)S(1)} %bitcast.9, bf16[16,2048]{1,0:T(8,128)(2,1)S(1)} %dynamic-slice_bitcast_fusion.own_ref, bf16[4096,256]{1,0:T(8,128)(2,1)S(1)} %copy-done), custom_call_target="tpu_custom_call" | custom-call | flops 268435456 | bytes 6291456 | tf_op jit(solution)/shard_map/pallas_call | solution.py:163
  49.7 0.0 copy-start.1
  49.7 0.0 all-to-all-done
  49.7 1.8 %shard_map.49 = bf16[512,256]{1,0:T(8,128)(2,1)S(1)} custom-call(bf16[2,64,2048]{2,1,0:T(8,128)(2,1)S(1)} %bitcast.10, bf16[64,2048]{1,0:T(8,128)(2,1)S(1)} %bitcast.12, bf16[128,256]{1,0:T(8,128)(2,1)S(1)} %shard_map.48.own_part_ref, bf16[4096,256]{1,0:T(8,128)(2,1)S(1)} %copy-done), custom_call_target="tpu_custom_call" | custom-call | flops 805306368 | bytes 6291456 | tf_op jit(solution)/shard_map/pallas_call | solution.py:163
  51.5 14.4 %all_to_all.10 = bf16[16,32,256]{2,1,0:T(8,128)(2,1)S(1)} all-to-all(bf16[16,32,256]{2,1,0:T(8,128)(2,1)S(1)} %bitcast.13), channel_id=1, replica_groups=mesh['zl'=8,'x'=4,'core'=2,'y'=4,'zh'=2] {'x','y'}, dimensions={0} | all-to-all | bytes 524288 | tf_op jit(solution)/shard_map/all_to_all | solution.py:226
  65.9 0.0 copy-done.1
  65.9 0.7 %shard_map.50 = bf16[4,32,256]{2,1,0:T(8,128)(2,1)} custom-call(s32[1,64]{1,0:T(1,128)S(1)} %copy-done.1, bf16[512,256]{1,0:T(8,128)(2,1)S(1)} %bitcast.14), custom_call_target="tpu_custom_call" | custom-call | tf_op jit(solution)/shard_map/pallas_call | solution.py:204
  (1 shorter events, 0.0 us)
Async XLA Ops:
  0.0 48.9 %copy-start = (bf16[4096,256]{1,0:T(8,128)(2,1)S(1)}, bf16[4096,256]{1,0:T(8,128)(2,1)}, u32[]{:S(2)}) copy-start(bf16[4096,256]{1,0:T(8,128)(2,1)} %constant.12.clone.table) | copy-start | bytes 6291460
  34.4 15.3 %all-to-all-start = ((bf16[4,16,2048]{2,1,0:T(8,128)(2,1)}), bf16[4,16,2048]{2,1,0:T(8,128)(2,1)S(1)}, u32[]{:S(2)}, u32[]{:S(2)}) async-start(bf16[4,16,2048]{2,1,0:T(8,128)(2,1)} %broadcast_in_dim.8.sent_ref), calls=%async_computation | async-start | bytes 524288 | tf_op jit(solution)/shard_map/all_to_all | solution.py:219
  49.7 16.2 %copy-start.1 = (s32[1,64]{1,0:T(1,128)S(1)}, s32[1,64]{1,0:T(1,128)}, u32[]{:S(2)}) copy-start(s32[1,64]{1,0:T(1,128)} %mask_ref.1) | copy-start | bytes 772

commit v7 on v6

--- a/solution.py
+++ b/solution.py
@@ -33,14 +33,13 @@
     return both.astype(ml_dtypes.bfloat16)
 
 
-def whiten_kernel(quality_ref, spectra_ref, white_ref):
-    re = spectra_ref[0, 0].astype(jnp.float32)
-    im = spectra_ref[1, 0].astype(jnp.float32)
+def whiten_kernel(quality_ref, values_ref, white_ref):
+    re, im = values_ref[0, 0], values_ref[1, 0]
     power_mean = jnp.mean(re * re + im * im, axis=-1, keepdims=True)
-    row = lax.broadcasted_iota(jnp.int32, (4, 1), 0)
-    flags = jnp.zeros((4, 1), jnp.float32)
-    for s in range(4):
-        flags = jnp.where(row == s, quality_ref[0, s].astype(jnp.float32), flags)
+    row = lax.broadcasted_iota(jnp.int32, (4, 4), 0)
+    column = lax.broadcasted_iota(jnp.int32, (4, 4), 1)
+    quality = jnp.broadcast_to(quality_ref[...].astype(jnp.float32), (4, 4))
+    flags = jnp.sum(jnp.where(row == column, quality, 0.0), axis=1, keepdims=True)
     scale = lax.rsqrt(power_mean + 1e-06) * flags
     white_ref[...] = jnp.concatenate([re * scale, im * scale], axis=0).astype(jnp.bfloat16)
 
@@ -49,9 +48,10 @@
     return pl.pallas_call(
         whiten_kernel,
         out_shape=jax.ShapeDtypeStruct((8, BINS), jnp.bfloat16),
-        in_specs=[SMEM, VMEM],
-        out_specs=VMEM,
-    )(quality, spectra)
+        in_specs=[VMEM, VMEM],
+        out_specs=VMEM,
+        compiler_params=SMALL,
+    )(quality, spectra.astype(jnp.float32))
 
 
 def choose_kernel(column_ref, sent_ref, chosen_ref):

time: 67.2 us -> 67 us (level)
  Pallas kernels: 5.06 us -> 3.52 us
  other arithmetic: 0 us -> 0.91 us
    pallas_call x1, Pallas kernels: 1.65 us -> 0.11 us  [whiten(): pl.pallas_call(whiten_kernel, out_shape=jax.ShapeDtypeStruct((8, BINS), j...]
    convert_element_type x0 -> x1, other arithmetic: none -> 0.91 us  [whiten(): spectra.astype(jnp.float32)]
where the time goes in v7:
time: 67 us; the launch traced here: 66.4 us
  blocking collectives  56.5 us (84%)
  starting transfers between devices  4.01 us (6%)
  Pallas kernels  3.52 us (5%)
  local copies, waits for them, and re-layouts  1.38 us (2%)
  other arithmetic  0.91 us (1%)
    all_gather x1, blocking collectives, shards(): column = lax.all_gather(white, ('zh', 'zl'))  31.8 us
    all_to_all x1, blocking collectives, shards(): lax.all_to_all(partial.reshape(16, 32, LAGS), ('x', 'y'), 0, 0, tiled=True)  14.4 us
    all_gather x1, blocking collectives, shards(): far = lax.all_gather(mine, 'core')  10.3 us
    all_to_all x1, starting transfers between devices, shards(): plane = lax.all_to_all(copies, 'x', 0, 0, tiled=True)  4.01 us
    pallas_call x2, Pallas kernels, pairs(): pl.pallas_call(kernel, out_shape=jax.ShapeDtypeStruct((result_rows, LAGS)...  2.59 us
  transfers between devices with their start and end apart: 1, of which 0 were waited for; matrix products, arithmetic and copies ran while one was open for 0% of the time, Pallas kernels for 1%

profile of v7, /device:TPU:1, one launch (start us, length us, event | category | flops | bytes accessed | tf_op | source)
XLA Modules:
  0.0 66.4 jit_solution(14227234699387318400)
XLA Ops:
  0.0 0.0 copy-start
  0.0 0.9 %convert_element_type.3.values_ref = f32[2,1,4,2048]{3,2,1,0:T(4,128)S(1)} convert(bf16[2,1,4,2048]{3,2,1,0:T(4,128)(2,1)} %param.4) | non-fusion elementwise | flops 16384 | bytes 98304 | tf_op jit(solution)/shard_map/convert_element_type | solution.py:54
  0.9 0.0 copy-start.1
  0.9 0.7 copy-done.1
  1.6 0.1 shard_map.46
  1.7 31.8 %all-gather.column_ref = bf16[128,2048]{1,0:T(8,128)(2,1)S(1)} all-gather(bf16[8,2048]{1,0:T(8,128)(2,1)S(1)} %shard_map.46), channel_id=2, replica_groups=mesh['zl'=8,'x'=4,'core'=2,'y'=4,'zh'=2] {'zh','zl'}, dimensions={0}, use_global_device_ids=true | all-gather | bytes 557056 | tf_op jit(solution)/shard_map/all_gather | solution.py:215
  33.5 0.7 %broadcast_in_dim.8.sent_ref = bf16[4,16,2048]{2,1,0:T(8,128)(2,1)} broadcast(bf16[16,2048]{1,0:T(8,128)(2,1)S(1)} %dynamic-slice_bitcast_fusion.own_ref), dimensions={1,2} | broadcast | bytes 327680 | tf_op jit(solution)/shard_map/broadcast_in_dim | solution.py:218
  34.2 4.0 %all-to-all-start = ((bf16[4,16,2048]{2,1,0:T(8,128)(2,1)}), bf16[4,16,2048]{2,1,0:T(8,128)(2,1)S(1)}, u32[]{:S(2)}, u32[]{:S(2)}) async-start(bf16[4,16,2048]{2,1,0:T(8,128)(2,1)} %broadcast_in_dim.8.sent_ref), calls=%async_computation | async-start | bytes 524288 | tf_op jit(solution)/shard_map/all_to_all | solution.py:219
  38.2 0.1 shard_map.47
  38.3 10.3 %all-gather.1 = bf16[128,2048]{1,0:T(8,128)(2,1)S(1)} all-gather(bf16[64,2048]{1,0:T(8,128)(2,1)S(1)} %shard_map.47), channel_id=3, replica_groups=mesh['zl'=8,'x'=4,'core'=2,'y'=4,'zh'=2] {'core'}, dimensions={0}, use_global_device_ids=true | all-gather | bytes 786432 | tf_op jit(solution)/shard_map/all_gather | solution.py:221
  48.6 0.0 copy-done
  48.6 0.8 %shard_map.48.own_part_ref = bf16[128,256]{1,0:T(8,128)(2,1)S(1)} custom-call(bf16[2,64,2048]{2,1,0:T(8,128)(2,1)S(1)} %bitcast.9, bf16[16,2048]{1,0:T(8,128)(2,1)S(1)} %dynamic-slice_bitcast_fusion.own_ref, bf16[4096,256]{1,0:T(8,128)(2,1)S(1)} %copy-done), custom_call_target="tpu_custom_call" | custom-call | flops 268435456 | bytes 6291456 | tf_op jit(solution)/shard_map/pallas_call | solution.py:163
  49.5 0.0 copy-start.2
  49.5 0.0 all-to-all-done
  49.5 1.8 %shard_map.49 = bf16[512,256]{1,0:T(8,128)(2,1)S(1)} custom-call(bf16[2,64,2048]{2,1,0:T(8,128)(2,1)S(1)} %bitcast.10, bf16[64,2048]{1,0:T(8,128)(2,1)S(1)} %bitcast.12, bf16[128,256]{1,0:T(8,128)(2,1)S(1)} %shard_map.48.own_part_ref, bf16[4096,256]{1,0:T(8,128)(2,1)S(1)} %copy-done), custom_call_target="tpu_custom_call" | custom-call | flops 805306368 | bytes 6291456 | tf_op jit(solution)/shard_map/pallas_call | solution.py:163
  51.3 14.4 %all_to_all.10 = bf16[16,32,256]{2,1,0:T(8,128)(2,1)S(1)} all-to-all(bf16[16,32,256]{2,1,0:T(8,128)(2,1)S(1)} %bitcast.13), channel_id=1, replica_groups=mesh['zl'=8,'x'=4,'core'=2,'y'=4,'zh'=2] {'x','y'}, dimensions={0} | all-to-all | bytes 524288 | tf_op jit(solution)/shard_map/all_to_all | solution.py:226
  65.7 0.0 copy-done.2
  65.7 0.7 %shard_map.50 = bf16[4,32,256]{2,1,0:T(8,128)(2,1)} custom-call(s32[1,64]{1,0:T(1,128)S(1)} %copy-done.2, bf16[512,256]{1,0:T(8,128)(2,1)S(1)} %bitcast.14), custom_call_target="tpu_custom_call" | custom-call | tf_op jit(solution)/shard_map/pallas_call | solution.py:204
  (1 shorter events, 0.0 us)
Async XLA Ops:
  0.0 48.6 %copy-start = (bf16[4096,256]{1,0:T(8,128)(2,1)S(1)}, bf16[4096,256]{1,0:T(8,128)(2,1)}, u32[]{:S(2)}) copy-start(bf16[4096,256]{1,0:T(8,128)(2,1)} %constant.12.clone.table) | copy-start | bytes 6291460
  0.9 0.7 copy-start.1
  34.2 15.3 %all-to-all-start = ((bf16[4,16,2048]{2,1,0:T(8,128)(2,1)}), bf16[4,16,2048]{2,1,0:T(8,128)(2,1)S(1)}, u32[]{:S(2)}, u32[]{:S(2)}) async-start(bf16[4,16,2048]{2,1,0:T(8,128)(2,1)} %broadcast_in_dim.8.sent_ref), calls=%async_computation | async-start | bytes 524288 | tf_op jit(solution)/shard_map/all_to_all | solution.py:219
  49.5 16.2 %copy-start.2 = (s32[1,64]{1,0:T(1,128)S(1)}, s32[1,64]{1,0:T(1,128)}, u32[]{:S(2)}) copy-start(s32[1,64]{1,0:T(1,128)} %mask_ref.1) | copy-start | bytes 772

commit v8 on v7

--- a/solution.py
+++ b/solution.py
@@ -33,8 +33,9 @@
     return both.astype(ml_dtypes.bfloat16)
 
 
-def whiten_kernel(quality_ref, values_ref, white_ref):
-    re, im = values_ref[0, 0], values_ref[1, 0]
+def whiten_kernel(quality_ref, spectra_ref, white_ref):
+    re = spectra_ref[0, 0].astype(jnp.float32)
+    im = spectra_ref[1, 0].astype(jnp.float32)
     power_mean = jnp.mean(re * re + im * im, axis=-1, keepdims=True)
     row = lax.broadcasted_iota(jnp.int32, (4, 4), 0)
     column = lax.broadcasted_iota(jnp.int32, (4, 4), 1)
@@ -50,8 +51,7 @@
         out_shape=jax.ShapeDtypeStruct((8, BINS), jnp.bfloat16),
         in_specs=[VMEM, VMEM],
         out_specs=VMEM,
-        compiler_params=SMALL,
-    )(quality, spectra.astype(jnp.float32))
+    )(quality, spectra)
 
 
 def choose_kernel(column_ref, sent_ref, chosen_ref):
@@ -77,8 +77,6 @@
 
 
 def correlate(stations, far, own, crosses, total, table):
-    total[...] = jnp.zeros_like(total)
-
     def products(step, cross):
         for part in range(STEP):
             bins = pl.ds(pl.multiple_of((step * STEP + part) * CHUNK, CHUNK), CHUNK)
@@ -99,24 +97,23 @@
                     cross[to : to + 16, first : first + CHUNK] = re.astype(jnp.bfloat16)
                     cross[to : to + 16, first + CHUNK : first + 2 * CHUNK] = im.astype(jnp.bfloat16)
 
-    def to_lags(step, cross):
+    def lags(step, cross):
         depth = 2 * CHUNK * STEP
         rows = pl.ds(pl.multiple_of(step * depth, depth), depth)
-        total[...] += jnp.dot(cross[...], table[rows, :], preferred_element_type=jnp.float32)
+        return jnp.dot(cross[...], table[rows, :], preferred_element_type=jnp.float32)
+
+    def to_lags(step, cross):
+        total[...] += lags(step, cross)
 
     even, odd = crosses
     products(0, even)
 
-    @pl.loop(0, STEPS // 2 - 1)
-    def _(n):
-        products(2 * n + 1, odd)
-        to_lags(2 * n, even)
-        products(2 * n + 2, even)
-        to_lags(2 * n + 1, odd)
-
-    products(STEPS - 1, odd)
-    to_lags(STEPS - 2, even)
-    to_lags(STEPS - 1, odd)
+    products(1, odd)
+    total[...] = lags(0, even)
+    for n in range(2, STEPS):
+        products(n, crosses[n % 2])
+        to_lags(n - 1, crosses[(n - 1) % 2])
+    to_lags(STEPS - 1, crosses[(STEPS - 1) % 2])
 
 
 def reorder(stations, total, order):

time: 67 us -> 67.2 us (level)
  Pallas kernels: 3.52 us -> 5.07 us
  other arithmetic: 0.91 us -> 0 us
    pallas_call x1, Pallas kernels: 0.11 us -> 1.65 us  [whiten(): pl.pallas_call(whiten_kernel, out_shape=jax.ShapeDtypeStruct((8, BINS), j...]
    convert_element_type x1 -> x0, other arithmetic: 0.91 us -> none  [whiten(): spectra.astype(jnp.float32)]
where the time goes in v8:
time: 67.2 us; the launch traced here: 66.6 us
  blocking collectives  56.8 us (85%)
  Pallas kernels  5.07 us (8%)
  starting transfers between devices  4.01 us (6%)
  local copies, waits for them, and re-layouts  0.72 us (1%)
    all_gather x1, blocking collectives, shards(): column = lax.all_gather(white, ('zh', 'zl'))  32 us
    all_to_all x1, blocking collectives, shards(): lax.all_to_all(partial.reshape(16, 32, LAGS), ('x', 'y'), 0, 0, tiled=True)  14.4 us
    all_gather x1, blocking collectives, shards(): far = lax.all_gather(mine, 'core')  10.3 us
    all_to_all x1, starting transfers between devices, shards(): plane = lax.all_to_all(copies, 'x', 0, 0, tiled=True)  4.01 us
    pallas_call x2, Pallas kernels, pairs(): pl.pallas_call(kernel, out_shape=jax.ShapeDtypeStruct((result_rows, LAGS)...  2.59 us
    pallas_call x1, Pallas kernels, whiten(): pl.pallas_call(whiten_kernel, out_shape=jax.ShapeDtypeStruct((8, BINS), j...  1.65 us
  transfers between devices with their start and end apart: 1, of which 0 were waited for; matrix products, arithmetic and copies ran while one was open for 0% of the time, Pallas kernels for 1%

profile of v8, /device:TPU:1, one launch (start us, length us, event | category | flops | bytes accessed | tf_op | source)
XLA Modules:
  0.0 66.6 jit_solution(16598180377559827553)
XLA Ops:
  0.0 0.0 copy-start
  0.0 1.7 %shard_map.46 = bf16[8,2048]{1,0:T(8,128)(2,1)} custom-call(s32[1,4]{1,0:T(1,128)} %quality_ref.1, bf16[2,1,4,2048]{3,2,1,0:T(4,128)(2,1)} %spectra_ref.1), custom_call_target="tpu_custom_call" | custom-call | tf_op jit(solution)/shard_map/pallas_call | solution.py:49
  1.7 32.0 %all-gather.column_ref = bf16[128,2048]{1,0:T(8,128)(2,1)S(1)} all-gather(bf16[8,2048]{1,0:T(8,128)(2,1)} %shard_map.46), channel_id=2, replica_groups=mesh['zl'=8,'x'=4,'core'=2,'y'=4,'zh'=2] {'zh','zl'}, dimensions={0}, use_global_device_ids=true | all-gather | bytes 557056 | tf_op jit(solution)/shard_map/all_gather | solution.py:212
  33.7 0.7 %broadcast_in_dim.8.sent_ref = bf16[4,16,2048]{2,1,0:T(8,128)(2,1)} broadcast(bf16[16,2048]{1,0:T(8,128)(2,1)S(1)} %dynamic-slice_bitcast_fusion.own_ref), dimensions={1,2} | broadcast | bytes 327680 | tf_op jit(solution)/shard_map/broadcast_in_dim | solution.py:215
  34.4 4.0 %all-to-all-start = ((bf16[4,16,2048]{2,1,0:T(8,128)(2,1)}), bf16[4,16,2048]{2,1,0:T(8,128)(2,1)S(1)}, u32[]{:S(2)}, u32[]{:S(2)}) async-start(bf16[4,16,2048]{2,1,0:T(8,128)(2,1)} %broadcast_in_dim.8.sent_ref), calls=%async_computation | async-start | bytes 524288 | tf_op jit(solution)/shard_map/all_to_all | solution.py:216
  38.4 0.1 shard_map.47
  38.5 10.3 %all-gather.1 = bf16[128,2048]{1,0:T(8,128)(2,1)S(1)} all-gather(bf16[64,2048]{1,0:T(8,128)(2,1)S(1)} %shard_map.47), channel_id=3, replica_groups=mesh['zl'=8,'x'=4,'core'=2,'y'=4,'zh'=2] {'core'}, dimensions={0}, use_global_device_ids=true | all-gather | bytes 786432 | tf_op jit(solution)/shard_map/all_gather | solution.py:218
  48.9 0.0 copy-done
  48.9 0.8 %shard_map.48.own_part_ref = bf16[128,256]{1,0:T(8,128)(2,1)S(1)} custom-call(bf16[2,64,2048]{2,1,0:T(8,128)(2,1)S(1)} %bitcast.9, bf16[16,2048]{1,0:T(8,128)(2,1)S(1)} %dynamic-slice_bitcast_fusion.own_ref, bf16[4096,256]{1,0:T(8,128)(2,1)S(1)} %copy-done), custom_call_target="tpu_custom_call" | custom-call | flops 268435456 | bytes 6291456 | tf_op jit(solution)/shard_map/pallas_call | solution.py:160
  49.7 0.0 copy-start.1
  49.7 0.0 all-to-all-done
  49.7 1.8 %shard_map.49 = bf16[512,256]{1,0:T(8,128)(2,1)S(1)} custom-call(bf16[2,64,2048]{2,1,0:T(8,128)(2,1)S(1)} %bitcast.10, bf16[64,2048]{1,0:T(8,128)(2,1)S(1)} %bitcast.12, bf16[128,256]{1,0:T(8,128)(2,1)S(1)} %shard_map.48.own_part_ref, bf16[4096,256]{1,0:T(8,128)(2,1)S(1)} %copy-done), custom_call_target="tpu_custom_call" | custom-call | flops 805306368 | bytes 6291456 | tf_op jit(solution)/shard_map/pallas_call | solution.py:160
  51.5 14.4 %all_to_all.10 = bf16[16,32,256]{2,1,0:T(8,128)(2,1)S(1)} all-to-all(bf16[16,32,256]{2,1,0:T(8,128)(2,1)S(1)} %bitcast.13), channel_id=1, replica_groups=mesh['zl'=8,'x'=4,'core'=2,'y'=4,'zh'=2] {'x','y'}, dimensions={0} | all-to-all | bytes 524288 | tf_op jit(solution)/shard_map/all_to_all | solution.py:223
  65.9 0.0 copy-done.1
  65.9 0.7 %shard_map.50 = bf16[4,32,256]{2,1,0:T(8,128)(2,1)} custom-call(s32[1,64]{1,0:T(1,128)S(1)} %copy-done.1, bf16[512,256]{1,0:T(8,128)(2,1)S(1)} %bitcast.14), custom_call_target="tpu_custom_call" | custom-call | tf_op jit(solution)/shard_map/pallas_call | solution.py:201
  (1 shorter events, 0.0 us)
Async XLA Ops:
  0.0 48.9 %copy-start = (bf16[4096,256]{1,0:T(8,128)(2,1)S(1)}, bf16[4096,256]{1,0:T(8,128)(2,1)}, u32[]{:S(2)}) copy-start(bf16[4096,256]{1,0:T(8,128)(2,1)} %constant.12.clone.table) | copy-start | bytes 6291460
  34.4 15.3 %all-to-all-start = ((bf16[4,16,2048]{2,1,0:T(8,128)(2,1)}), bf16[4,16,2048]{2,1,0:T(8,128)(2,1)S(1)}, u32[]{:S(2)}, u32[]{:S(2)}) async-start(bf16[4,16,2048]{2,1,0:T(8,128)(2,1)} %broadcast_in_dim.8.sent_ref), calls=%async_computation | async-start | bytes 524288 | tf_op jit(solution)/shard_map/all_to_all | solution.py:216
  49.7 16.2 %copy-start.1 = (s32[1,64]{1,0:T(1,128)S(1)}, s32[1,64]{1,0:T(1,128)}, u32[]{:S(2)}) copy-start(s32[1,64]{1,0:T(1,128)} %mask_ref.1) | copy-start | bytes 772
